TPU v7x, 256 devices: a whole 4x4x8 slice. The times are simulated.
256 devices in a mesh: face: 8 (over z_hi, core), tile: 32 (over y, z_lo, x).
Axes of the slice: x: 4, y: 4, z: 8 (z_hi: 4, z_lo: 2; z = z_hi * 2 + z_lo), core: 2. Of those that a mesh axis runs over, the one named last changes fastest.
Arguments:
- activation: bfloat16 [16, 32, 24, 12, 128], P('face', 'tile'), may hold values from -6 to 6
- cotangent: bfloat16 [16, 32, 24, 12, 128], P('face', 'tile'), may hold values from -6 to 6
- weight_one: bfloat16 [9, 128, 128], replicated, may hold values from -0.1875 to 0.1875
- weight_two: bfloat16 [9, 128, 128], replicated, may hold values from -0.1875 to 0.1875
- weight_three: bfloat16 [9, 128, 128], replicated, may hold values from -0.1875 to 0.1875
- neighbor: int32 [12, 4], replicated, may hold values from 0 to 11, as said below
- turn: int32 [12, 4], replicated, may hold values from 0 to 7, as said below
Outputs:
- grad_input: bfloat16 [16, 32, 24, 12, 128], P('face', 'tile')
- grad_one: float32 [9, 128, 128], replicated
- grad_two: float32 [9, 128, 128], replicated
- grad_three: float32 [9, 128, 128], replicated
Inputs may be any that keep to these rules, and one draw needn't show every extreme that they name: Face f's edge e meets edge turn[f, e] % 4 of face neighbor[f, e]; the meeting is mutual: that edge meets edge e of f back, with the same turn // 4; every one of the 12 x 4 edges meets exactly one other edge. `turn`: edge numbers 0 first row, 1 last row, 2 first column, 3 last column; 4 is added where the cells meet in reversed order.
All inputs are finite; a program needn't handle non-finite values.
Results may differ from a plain program's by a relative error of at most 0.015.
Values may be sent and summed in bfloat16 or wider, within the bound.
A program may use at most 64 MiB of HBM per device.

v0:
```python
import math

import jax
import jax.numpy as jnp
from jax import lax
from jax.sharding import PartitionSpec as P

FACES = 12
TGR = 4


TAP_TABLE = ((0, 1, 2), (6, 7, 8), (0, 3, 6), (2, 5, 8))


def shortened(array):

    def short(part):
        return part.astype(jnp.bfloat16) if part.dtype == jnp.float32 else part

    return jax.tree.map(short, array)


def edge_strips(field):
    return (field[None, :, 0], field[None, :, -1], field[None, :, :, 0], field[None, :, :, -1])


def boundary_lines(strips, columns):
    tops, bottoms, lefts, rights = strips
    count = tops.shape[0]
    slots = tops.shape[1]
    chan = tops.shape[-1]

    def joined(stack):
        return jnp.moveaxis(stack, 0, 1).reshape(slots, -1, chan)

    lines = jnp.stack(
        [
            joined(tops[:columns]),
            joined(bottoms[count - columns :]),
            joined(lefts[0::columns]),
            joined(rights[columns - 1 :: columns]),
        ],
        axis=1,
    )
    return jnp.pad(lines, ((0, 0), (0, 0), (1, 1), (0, 0)))


def cycle_positions(slots, neighbor, turn, row, col, tile_h, tile_w, side, width):
    valid = slots < FACES
    chosen = (
        jnp.minimum(slots, FACES - 1)[:, None] == jnp.arange(FACES, dtype=jnp.int32)[None, :]
    ).astype(jnp.int32)
    source = jnp.sum(chosen[:, :, None] * neighbor[None], axis=1)
    code = jnp.sum(chosen[:, :, None] * turn[None], axis=1)
    edge_code = code % 4
    reverse = code // 4
    starts = jnp.stack([col * tile_w, col * tile_w, row * tile_h, row * tile_h]) - 1
    spans = jnp.array([tile_w, tile_w, tile_h, tile_h], jnp.int32) + 2
    offset = jnp.arange(width, dtype=jnp.int32)
    along = starts[:, None] + offset[None, :]
    inside = offset[None, :] < spans[:, None]
    mapped = jnp.where(reverse[:, :, None] == 1, side - 1 - along[None], along[None]) + 1
    keep = inside[None] & valid[:, None, None]
    place = jnp.where(keep, mapped, 0)
    return (source, edge_code, place, reverse, valid)


def pick_segments(flat, source, edge_code, place, side):
    index = (source[:, :, None] * 4 + edge_code[:, :, None]) * (side + 2) + place
    values = jnp.take(flat, index.reshape(-1), axis=0)
    return values.reshape(index.shape + (flat.shape[-1],))


def assemble(field, strips, segments, row, col, columns, rows):
    tops, bottoms, lefts, rights = strips
    count = tops.shape[0]
    tile_h, tile_w = (field.shape[1], field.shape[2])
    here = row * columns + col

    def pick(stack, index):
        return lax.dynamic_index_in_dim(stack, jnp.clip(index, 0, count - 1), 0, keepdims=False)

    above_left = jnp.where(col > 0, pick(bottoms, here - columns - 1)[:, -1], segments[:, 2, 0])
    above_right = jnp.where(
        col < columns - 1, pick(bottoms, here - columns + 1)[:, 0], segments[:, 3, 0]
    )
    inner_top = jnp.concatenate(
        [above_left[:, None], pick(bottoms, here - columns), above_right[:, None]], axis=1
    )
    top_row = jnp.where(row == 0, segments[:, 0, : tile_w + 2], inner_top)
    below_left = jnp.where(
        col > 0, pick(tops, here + columns - 1)[:, -1], segments[:, 2, tile_h + 1]
    )
    below_right = jnp.where(
        col < columns - 1, pick(tops, here + columns + 1)[:, 0], segments[:, 3, tile_h + 1]
    )
    inner_bottom = jnp.concatenate(
        [below_left[:, None], pick(tops, here + columns), below_right[:, None]], axis=1
    )
    bottom_row = jnp.where(row == rows - 1, segments[:, 1, : tile_w + 2], inner_bottom)
    left_col = jnp.where(col == 0, segments[:, 2, 1 : tile_h + 1], pick(rights, here - 1))
    right_col = jnp.where(col == columns - 1, segments[:, 3, 1 : tile_h + 1], pick(lefts, here + 1))
    middle = jnp.concatenate([left_col[:, :, None], field, right_col[:, :, None]], axis=2)
    return jnp.concatenate([top_row[:, None], middle, bottom_row[:, None]], axis=1)


def conv_forward(padded, weight):
    count, tile_h, tile_w = (padded.shape[0], padded.shape[1] - 2, padded.shape[2] - 2)
    total = jnp.zeros((count * tile_h * tile_w, weight.shape[-1]), jnp.float32)
    for dy in range(3):
        for dx in range(3):
            window = padded[:, dy : dy + tile_h, dx : dx + tile_w].reshape(-1, padded.shape[-1])
            total = total + jnp.dot(window, weight[3 * dy + dx], preferred_element_type=jnp.float32)
    return total.reshape(count, tile_h, tile_w, -1)


def conv_backward(extended, weight):
    count, tile_h, tile_w = (extended.shape[0], extended.shape[1] - 2, extended.shape[2] - 2)
    total = jnp.zeros((count * tile_h * tile_w, weight.shape[1]), jnp.float32)
    for dy in range(3):
        for dx in range(3):
            window = extended[:, 2 - dy : 2 - dy + tile_h, 2 - dx : 2 - dx + tile_w].reshape(
                -1, extended.shape[-1]
            )
            total = total + lax.dot_general(
                window,
                weight[3 * dy + dx],
                (((1,), (1,)), ((), ())),
                preferred_element_type=jnp.float32,
            )
    return total.reshape(count, tile_h, tile_w, -1)


def weight_grad(padded, grad):
    tile_h, tile_w = (grad.shape[1], grad.shape[2])
    flat_grad = grad.reshape(-1, grad.shape[-1])
    parts = []
    for dy in range(3):
        for dx in range(3):
            window = padded[:, dy : dy + tile_h, dx : dx + tile_w].reshape(-1, padded.shape[-1])
            parts.append(
                lax.dot_general(
                    window, flat_grad, (((0,), (0,)), ((), ())), preferred_element_type=jnp.float32
                )
            )
    return jnp.stack(parts)


def cross_face(segments, weight, edge_code, reverse):
    width = segments.shape[2]
    taps = jnp.array(TAP_TABLE, jnp.int32)
    code_hot = (edge_code[:, :, None] == jnp.arange(4, dtype=jnp.int32)).astype(jnp.int32)
    tap_ids = jnp.sum(code_hot[:, :, :, None] * taps[None, None], axis=2)
    tap_hot = (tap_ids[..., None] == jnp.arange(9, dtype=jnp.int32)).astype(jnp.float32)
    selected = jnp.einsum("sedk,kcf->sedcf", tap_hot, weight.astype(jnp.float32)).astype(
        weight.dtype
    )
    total = jnp.zeros(segments.shape[:2] + (width - 2, weight.shape[1]), jnp.float32)
    for step in range(3):
        lean = 1 - step
        ahead = segments[:, :, 1 + lean : width - 1 + lean]
        behind = segments[:, :, 1 - lean : width - 1 - lean]
        chosen = jnp.where(reverse[:, :, None, None] == 1, behind, ahead)
        total = total + jnp.einsum(
            "sejf,secf->sejc", chosen, selected[:, :, step], preferred_element_type=jnp.float32
        )
    return total


def shards(activation, cotangent, weight_one, weight_two, weight_three, neighbor, turn):
    slots_here = activation.shape[0]
    tile_h, tile_w, chan = (activation.shape[2], activation.shape[3], activation.shape[4])
    columns = lax.axis_size("tile") // TGR
    side = tile_h * TGR
    width = max(tile_h, tile_w) + 2
    face_id = lax.axis_index("face")
    tile_id = lax.axis_index("tile")
    row = tile_id // columns
    col = tile_id % columns
    mine = face_id * slots_here + jnp.arange(slots_here, dtype=jnp.int32)
    alive = (mine < FACES)[:, None, None, None]
    source, edge_code, place, reverse, valid = cycle_positions(
        mine, neighbor, turn, row, col, tile_h, tile_w, side, width
    )

    def pull(lines):
        everyone = lax.all_gather(lines, "face", axis=0, tiled=True)
        return pick_segments(everyone.reshape(-1, chan), source, edge_code, place, side)

    def halo(field, outer):
        strips = lax.all_gather(shortened(edge_strips(field)), "tile", axis=0, tiled=True)
        segments = pull(boundary_lines(strips, columns))
        cycle = segments if outer else jnp.zeros_like(segments)
        return (assemble(field, strips, cycle, row, col, columns, TGR), segments)

    def backward(delta, weight):
        extended, segments = halo(delta, False)
        grad = conv_backward(extended, weight)
        cycle_grad = cross_face(segments, weight, edge_code, reverse)
        grad = grad.at[:, 0].add(jnp.where(row == 0, cycle_grad[:, 0, :tile_w], 0.0))
        grad = grad.at[:, -1].add(jnp.where(row == TGR - 1, cycle_grad[:, 1, :tile_w], 0.0))
        grad = grad.at[:, :, 0].add(jnp.where(col == 0, cycle_grad[:, 2, :tile_h], 0.0))
        grad = grad.at[:, :, -1].add(jnp.where(col == columns - 1, cycle_grad[:, 3, :tile_h], 0.0))
        return grad

    def gelu_back(pre, grad):
        unused, pullback = jax.vjp(jax.nn.gelu, pre)
        return pullback(grad)[0]

    def summed(grad):
        return lax.psum(grad, ("face", "tile"))

    scale = 1.0 / math.sqrt(FACES * side * side)
    inputs = jnp.where(alive, activation[:, 0], jnp.zeros_like(activation[:, 0]))
    upstream = jnp.where(alive, cotangent[:, 0], jnp.zeros_like(cotangent[:, 0])).astype(
        jnp.float32
    )
    padded_zero, unused_zero = halo(inputs, True)
    pre_one = conv_forward(padded_zero, weight_one)
    hidden_one = jax.nn.gelu(pre_one).astype(jnp.bfloat16)
    padded_one, unused_one = halo(hidden_one, True)
    pre_two = conv_forward(padded_one, weight_two)
    hidden_two = jax.nn.gelu(pre_two).astype(jnp.bfloat16)
    padded_two, unused_two = halo(hidden_two, True)
    pre_three = conv_forward(padded_two, weight_three)
    delta_three = gelu_back(pre_three, upstream).astype(jnp.bfloat16)
    grad_three = weight_grad(padded_two, delta_three)
    grad_three = summed(grad_three)
    delta_two = gelu_back(pre_two, backward(delta_three, weight_three)).astype(jnp.bfloat16)
    grad_two = weight_grad(padded_one, delta_two)
    grad_two = summed(grad_two)
    delta_one = gelu_back(pre_one, backward(delta_two, weight_two)).astype(jnp.bfloat16)
    grad_one = weight_grad(padded_zero, delta_one)
    grad_one = summed(grad_one)
    grad_input = backward(delta_one, weight_one).astype(jnp.bfloat16)
    return (grad_input[:, None], grad_one * scale, grad_two * scale, grad_three * scale)


def solution(mesh):
    return jax.shard_map(
        shards,
        mesh=mesh,
        in_specs=(
            P("face", "tile", None, None, None),
            P("face", "tile", None, None, None),
            P(),
            P(),
            P(),
            P(),
            P(),
        ),
        out_specs=(P("face", "tile", None, None, None), P(), P(), P()),
        check_vma=False,
    )
```

profile of v0, /device:TPU:1, one launch (start us, length us, event | category | flops | bytes accessed | tf_op | source)
XLA Modules:
  0.0 2435.1 jit_solution(3339274804377164482)
XLA Ops:
  8.3 70.0 %all-gather.1 = bf16[64,1,12,128]{3,2,1,0:T(8,128)(2,1)S(1)} all-gather(bf16[2,1,12,128]{3,2,1,0:T(8,128)(2,1)S(1)} %copy.8894), channel_id=3, replica_groups=mesh['face'=8,'tile'=32] {'tile'}, dimensions={0}, use_global_device_ids=true | all-gather | bytes 202752 | tf_op jit(solution)/shard_map/all_gather | solution.py:191
  78.4 63.2 %all-gather = bf16[64,1,12,128]{3,2,1,0:T(8,128)(2,1)S(1)} all-gather(bf16[2,1,12,128]{3,2,1,0:T(8,128)(2,1)S(1)} %copy.8891), channel_id=2, replica_groups=mesh['face'=8,'tile'=32] {'tile'}, dimensions={0}, use_global_device_ids=true | all-gather | bytes 202752 | tf_op jit(solution)/shard_map/all_gather | solution.py:191
  141.8 65.3 %all-gather.3 = bf16[64,24,1,128]{3,1,2,0:T(8,128)(2,1)S(1)} all-gather(bf16[2,24,1,128]{3,1,2,0:T(8,128)(2,1)S(1)} %get-tuple-element.419), channel_id=5, replica_groups=mesh['face'=8,'tile'=32] {'tile'}, dimensions={0}, use_global_device_ids=true | all-gather | bytes 405504 | tf_op jit(solution)/shard_map/all_gather | solution.py:191
  207.2 63.7 %all-gather.2 = bf16[64,24,1,128]{3,1,2,0:T(8,128)(2,1)S(1)} all-gather(bf16[2,24,1,128]{3,1,2,0:T(8,128)(2,1)S(1)} %get-tuple-element.420), channel_id=4, replica_groups=mesh['face'=8,'tile'=32] {'tile'}, dimensions={0}, use_global_device_ids=true | all-gather | bytes 405504 | tf_op jit(solution)/shard_map/all_gather | solution.py:191
  275.7 83.7 %all-gather.31.cloned.1.call-done = bf16[16,4,98,128]{3,1,2,0:T(4,128)(2,1)} async-done(((bf16[2,4,98,128]{3,1,2,0:T(4,128)(2,1)}), bf16[16,4,98,128]{3,1,2,0:T(4,128)(2,1)}) %all-gather.31.cloned.1.call-update) | async-done | bytes 1605648 | tf_op jit(solution)/shard_map/all_gather | solution.py:187
  368.2 68.7 %all-gather.5 = bf16[64,1,12,128]{3,2,1,0:T(8,128)(2,1)S(1)} all-gather(bf16[2,1,12,128]{3,2,1,0:T(8,128)(2,1)S(1)} %copy.8934), channel_id=7, replica_groups=mesh['face'=8,'tile'=32] {'tile'}, dimensions={0}, use_global_device_ids=true | all-gather | bytes 202752 | tf_op jit(solution)/shard_map/all_gather | solution.py:191
  500.0 65.2 %all-gather.7 = bf16[64,24,1,128]{3,1,2,0:T(8,128)(2,1)S(1)} all-gather(bf16[2,24,1,128]{3,1,2,0:T(8,128)(2,1)S(1)} %get-tuple-element.413), channel_id=9, replica_groups=mesh['face'=8,'tile'=32] {'tile'}, dimensions={0}, use_global_device_ids=true | all-gather | bytes 405504 | tf_op jit(solution)/shard_map/all_gather | solution.py:191
  565.2 63.7 %all-gather.6 = bf16[64,24,1,128]{3,1,2,0:T(8,128)(2,1)S(1)} all-gather(bf16[2,24,1,128]{3,1,2,0:T(8,128)(2,1)S(1)} %get-tuple-element.414), channel_id=8, replica_groups=mesh['face'=8,'tile'=32] {'tile'}, dimensions={0}, use_global_device_ids=true | all-gather | bytes 405504 | tf_op jit(solution)/shard_map/all_gather | solution.py:191
  632.4 81.9 %all-gather.33.cloned.1.call-done = bf16[16,4,98,128]{3,1,2,0:T(4,128)(2,1)} async-done(((bf16[2,4,98,128]{3,1,2,0:T(4,128)(2,1)}), bf16[16,4,98,128]{3,1,2,0:T(4,128)(2,1)}) %all-gather.33.cloned.1.call-update) | async-done | bytes 1605648 | tf_op jit(solution)/shard_map/all_gather | solution.py:187
  725.1 68.7 %all-gather.9 = bf16[64,1,12,128]{3,2,1,0:T(8,128)(2,1)S(1)} all-gather(bf16[2,1,12,128]{3,2,1,0:T(8,128)(2,1)S(1)} %copy.8973), channel_id=11, replica_groups=mesh['face'=8,'tile'=32] {'tile'}, dimensions={0}, use_global_device_ids=true | all-gather | bytes 202752 | tf_op jit(solution)/shard_map/all_gather | solution.py:191
  857.0 65.2 %all-gather.11 = bf16[64,24,1,128]{3,1,2,0:T(8,128)(2,1)S(1)} all-gather(bf16[2,24,1,128]{3,1,2,0:T(8,128)(2,1)S(1)} %get-tuple-element.407), channel_id=13, replica_groups=mesh['face'=8,'tile'=32] {'tile'}, dimensions={0}, use_global_device_ids=true | all-gather | bytes 405504 | tf_op jit(solution)/shard_map/all_gather | solution.py:191
  922.2 63.7 %all-gather.10 = bf16[64,24,1,128]{3,1,2,0:T(8,128)(2,1)S(1)} all-gather(bf16[2,24,1,128]{3,1,2,0:T(8,128)(2,1)S(1)} %get-tuple-element.408), channel_id=12, replica_groups=mesh['face'=8,'tile'=32] {'tile'}, dimensions={0}, use_global_device_ids=true | all-gather | bytes 405504 | tf_op jit(solution)/shard_map/all_gather | solution.py:191
  997.4 73.1 %all-gather.35.cloned.1.call-done = bf16[16,4,98,128]{3,1,2,0:T(4,128)(2,1)} async-done(((bf16[2,4,98,128]{3,1,2,0:T(4,128)(2,1)}), bf16[16,4,98,128]{3,1,2,0:T(4,128)(2,1)}) %all-gather.35.cloned.1.call-update) | async-done | bytes 1605648 | tf_op jit(solution)/shard_map/all_gather | solution.py:187
  1091.2 69.3 %all-gather.12 = bf16[64,24,1,128]{3,1,2,0:T(8,128)(2,1)S(1)} all-gather(bf16[2,24,1,128]{3,1,2,0:T(8,128)(2,1)S(1)} %get-tuple-element.401), channel_id=14, replica_groups=mesh['face'=8,'tile'=32] {'tile'}, dimensions={0}, use_global_device_ids=true | all-gather | bytes 405504 | tf_op jit(solution)/shard_map/all_gather | solution.py:191
  1161.1 63.4 %all-gather.13 = bf16[64,24,1,128]{3,1,2,0:T(8,128)(2,1)S(1)} all-gather(bf16[2,24,1,128]{3,1,2,0:T(8,128)(2,1)S(1)} %get-tuple-element.402), channel_id=15, replica_groups=mesh['face'=8,'tile'=32] {'tile'}, dimensions={0}, use_global_device_ids=true | all-gather | bytes 405504 | tf_op jit(solution)/shard_map/all_gather | solution.py:191
  1225.2 64.4 %all-gather.14 = bf16[64,1,12,128]{3,2,1,0:T(8,128)(2,1)S(1)} all-gather(bf16[2,1,12,128]{3,2,1,0:T(8,128)(2,1)S(1)} %copy.9011), channel_id=16, replica_groups=mesh['face'=8,'tile'=32] {'tile'}, dimensions={0}, use_global_device_ids=true | all-gather | bytes 202752 | tf_op jit(solution)/shard_map/all_gather | solution.py:191
  1457.3 69.1 %all-gather.16 = bf16[64,24,1,128]{3,1,2,0:T(8,128)(2,1)S(1)} all-gather(bf16[2,24,1,128]{3,1,2,0:T(8,128)(2,1)S(1)} %get-tuple-element.395), channel_id=18, replica_groups=mesh['face'=8,'tile'=32] {'tile'}, dimensions={0}, use_global_device_ids=true | all-gather | bytes 405504 | tf_op jit(solution)/shard_map/all_gather | solution.py:191
  1526.4 63.5 %all-gather.17 = bf16[64,24,1,128]{3,1,2,0:T(8,128)(2,1)S(1)} all-gather(bf16[2,24,1,128]{3,1,2,0:T(8,128)(2,1)S(1)} %get-tuple-element.396), channel_id=19, replica_groups=mesh['face'=8,'tile'=32] {'tile'}, dimensions={0}, use_global_device_ids=true | all-gather | bytes 405504 | tf_op jit(solution)/shard_map/all_gather | solution.py:191
  1590.0 65.0 %all-gather.18 = bf16[64,1,12,128]{3,2,1,0:T(8,128)(2,1)S(1)} all-gather(bf16[2,1,12,128]{3,2,1,0:T(8,128)(2,1)S(1)} %copy.9057), channel_id=20, replica_groups=mesh['face'=8,'tile'=32] {'tile'}, dimensions={0}, use_global_device_ids=true | all-gather | bytes 202752 | tf_op jit(solution)/shard_map/all_gather | solution.py:191
  1726.1 76.7 %all-gather.39.cloned.1.call-done = bf16[16,4,98,128]{3,1,2,0:T(4,128)(2,1)} async-done(((bf16[2,4,98,128]{3,1,2,0:T(4,128)(2,1)}), bf16[16,4,98,128]{3,1,2,0:T(4,128)(2,1)}) %all-gather.39.cloned.1.call-update) | async-done | bytes 1605648 | tf_op jit(solution)/shard_map/all_gather | solution.py:187
  1811.1 69.0 %all-gather.20 = bf16[64,24,1,128]{3,1,2,0:T(8,128)(2,1)S(1)} all-gather(bf16[2,24,1,128]{3,1,2,0:T(8,128)(2,1)S(1)} %get-tuple-element.389), channel_id=22, replica_groups=mesh['face'=8,'tile'=32] {'tile'}, dimensions={0}, use_global_device_ids=true | all-gather | bytes 405504 | tf_op jit(solution)/shard_map/all_gather | solution.py:191
  1943.6 64.9 %all-gather.23 = bf16[64,1,12,128]{3,2,1,0:T(8,128)(2,1)S(1)} all-gather(bf16[2,1,12,128]{3,2,1,0:T(8,128)(2,1)S(1)} %copy.9116), channel_id=25, replica_groups=mesh['face'=8,'tile'=32] {'tile'}, dimensions={0}, use_global_device_ids=true | all-gather | bytes 202752 | tf_op jit(solution)/shard_map/all_gather | solution.py:191
  2008.7 63.9 %all-gather.21 = bf16[64,24,1,128]{3,1,2,0:T(8,128)(2,1)S(1)} all-gather(bf16[2,24,1,128]{3,1,2,0:T(8,128)(2,1)S(1)} %get-tuple-element.390), channel_id=23, replica_groups=mesh['face'=8,'tile'=32] {'tile'}, dimensions={0}, use_global_device_ids=true | all-gather | bytes 405504 | tf_op jit(solution)/shard_map/all_gather | solution.py:191
  2080.6 304.2 %all-reduce.9.cloned.1.call-done = (f32[9,128,128]{2,1,0:T(8,128)}, f32[9,128,128]{2,1,0:T(8,128)}, f32[9,128,128]{2,1,0:T(8,128)}) async-done(((f32[9,128,128]{2,1,0:T(8,128)}, f32[9,128,128]{2,1,0:T(8,128)}, f32[9,128,128]{2,1,0:T(8,128)}), (f32[9,128,128]{2,1,0:T(8,128)}, f32[9,128,128]{2,1,0:T(8,128)}, f32[9,128,128]{2,1,0:T(8,128)})) %all-reduce.9.cloned.1.call-update) | async-done | bytes 1769488 | tf_op jit(solution)/shard_map/psum | solution.py:211
  (699 shorter events, 547.7 us)
Async XLA Ops:
  7.2 352.2 %all-gather.31.cloned.1.call-start = ((), (), s32[]{:S(2)}) async-start(), calls=%async_computation | async-start | bytes 1806336 | tf_op jit(solution)/shard_map/all_gather | solution.py:187
  7.2 266.4 %copy-start.59 = (pred[2]{0:T(512)(128)(4,1)}, pred[2]{0:T(512)(128)(4,1)S(1)}, u32[]{:S(2)}) copy-start(pred[2]{0:T(512)(128)(4,1)S(1)} %fusion.393) | copy-start | bytes 10
  141.7 130.8 %copy-start.64 = (s32[12,4]{0,1:T(4,128)S(1)}, s32[12,4]{0,1:T(4,128)}, u32[]{:S(2)}) copy-start(s32[12,4]{0,1:T(4,128)} %param.42) | copy-start | bytes 580
  141.7 130.8 %copy-start.65 = (s32[12,4]{0,1:T(4,128)S(1)}, s32[12,4]{0,1:T(4,128)}, u32[]{:S(2)}) copy-start(s32[12,4]{0,1:T(4,128)} %param.43) | copy-start | bytes 580
  141.7 130.9 %copy-start.74 = (s32[4]{0:T(128)S(1)}, s32[4]{0:T(128)}, u32[]{:S(2)}) copy-start(s32[4]{0:T(128)} %constant.524) | copy-start | bytes 52
  141.8 131.8 %copy-start.23 = (bf16[2,1,24,12,128]{4,2,3,1,0:T(8,128)(2,1)S(1)}, bf16[2,1,24,12,128]{4,2,3,1,0:T(8,128)(2,1)}, u32[]{:S(2)}) copy-start(bf16[2,1,24,12,128]{4,2,3,1,0:T(8,128)(2,1)} %param.37) | copy-start | bytes 442372
  207.1 67.3 %copy-start.35 = (bf16[64,24,1,128]{3,1,2,0:T(8,128)(2,1)}, bf16[64,24,1,128]{3,1,2,0:T(8,128)(2,1)S(1)}, u32[]{:S(2)}) copy-start(bf16[64,24,1,128]{3,1,2,0:T(8,128)(2,1)S(1)} %all-gather.3) | copy-start | bytes 1179652
  272.2 442.0 %all-gather.33.cloned.1.call-start = ((), (), s32[]{:S(2)}) async-start(), calls=%async_computation.1 | async-start | bytes 1806336 | tf_op jit(solution)/shard_map/all_gather | solution.py:187
  368.1 352.9 %copy-start.11 = (bf16[2,24,12,128]{3,1,2,0:T(8,128)(2,1)}, bf16[2,24,12,128]{3,1,2,0:T(8,128)(2,1)S(1)}, u32[]{:S(2)}) copy-start(bf16[2,24,12,128]{3,1,2,0:T(8,128)(2,1)S(1)} %multiply_convert_fusion.1) | copy-start | bytes 442372
  565.2 63.9 %copy-start.39 = (bf16[64,24,1,128]{3,1,2,0:T(8,128)(2,1)}, bf16[64,24,1,128]{3,1,2,0:T(8,128)(2,1)S(1)}, u32[]{:S(2)}) copy-start(bf16[64,24,1,128]{3,1,2,0:T(8,128)(2,1)S(1)} %all-gather.7) | copy-start | bytes 1179652
  631.0 439.5 %all-gather.35.cloned.1.call-start = ((), (), s32[]{:S(2)}) async-start(), calls=%async_computation.2 | async-start | bytes 1806336 | tf_op jit(solution)/shard_map/all_gather | solution.py:187
  724.8 269.4 %copy-start.16 = (bf16[576,128]{1,0:T(8,128)(2,1)}, bf16[576,128]{1,0:T(8,128)(2,1)S(1)}, u32[]{:S(2)}) copy-start(bf16[576,128]{1,0:T(8,128)(2,1)S(1)} %get-tuple-element.453) | copy-start | bytes 442372
  725.0 260.9 %copy-start.13 = (bf16[2,24,12,128]{3,1,2,0:T(8,128)(2,1)}, bf16[2,24,12,128]{3,1,2,0:T(8,128)(2,1)S(1)}, u32[]{:S(2)}) copy-start(bf16[2,24,12,128]{3,1,2,0:T(8,128)(2,1)S(1)} %multiply_convert_fusion) | copy-start | bytes 442372
  856.9 130.9 %copy-start.60 = (pred[2]{0:T(512)(128)(4,1)S(1)}, pred[2]{0:T(512)(128)(4,1)}, u32[]{:S(2)}) copy-start(pred[2]{0:T(512)(128)(4,1)} %copy-done.59) | copy-start | bytes 10
  856.9 131.7 %copy-start.24 = (bf16[2,1,24,12,128]{4,2,3,1,0:T(8,128)(2,1)S(1)}, bf16[2,1,24,12,128]{4,2,3,1,0:T(8,128)(2,1)}, u32[]{:S(2)}) copy-start(bf16[2,1,24,12,128]{4,2,3,1,0:T(8,128)(2,1)} %param.38) | copy-start | bytes 442372
  922.1 67.9 %copy-start.37 = (bf16[64,24,1,128]{3,1,2,0:T(8,128)(2,1)}, bf16[64,24,1,128]{3,1,2,0:T(8,128)(2,1)S(1)}, u32[]{:S(2)}) copy-start(bf16[64,24,1,128]{3,1,2,0:T(8,128)(2,1)S(1)} %all-gather.11) | copy-start | bytes 1179652
  922.1 67.2 %copy-start.63 = (s32[2,4]{1,0:T(2,128)S(1)}, s32[2,4]{1,0:T(2,128)}, u32[]{:S(2)}) copy-start(s32[2,4]{1,0:T(2,128)} %get-tuple-element.291) | copy-start | bytes 100
  922.1 67.2 %copy-start.66 = (s32[4,3]{0,1:T(4,128)S(1)}, s32[4,3]{0,1:T(4,128)}, u32[]{:S(2)}) copy-start(s32[4,3]{0,1:T(4,128)} %constant.509.clone) | copy-start | bytes 148
  987.3 452.6 %all-gather.37.cloned.1.call-start = ((), (), s32[]{:S(2)}) async-start(), calls=%async_computation.3 | async-start | bytes 1806336 | tf_op jit(solution)/shard_map/all_gather | solution.py:187
  1073.5 7.8 copy-start.14
  1356.0 446.9 %all-gather.39.cloned.1.call-start = ((), (), s32[]{:S(2)}) async-start(), calls=%async_computation.4 | async-start | bytes 1806336 | tf_op jit(solution)/shard_map/all_gather | solution.py:187
  1719.6 665.2 %all-reduce.9.cloned.1.call-start = ((), (), s32[]{:S(2)}) async-start(), calls=%async_computation.6 | async-start | bytes 3538944 | tf_op jit(solution)/shard_map/psum | solution.py:211
  1808.6 71.5 %copy-start.6 = (bf16[2,25,14,128]{3,1,2,0:T(8,128)(2,1)S(1)}, bf16[2,25,14,128]{3,1,2,0:T(8,128)(2,1)}, u32[]{:S(2)}) copy-start(bf16[2,25,14,128]{3,1,2,0:T(8,128)(2,1)} %copy-done.5) | copy-start | bytes 537604
  2075.5 344.7 %all-gather.41.cloned.1.call-start = ((), (), s32[]{:S(2)}) async-start(), calls=%async_computation.5 | async-start | bytes 1806336 | tf_op jit(solution)/shard_map/all_gather | solution.py:187
  (58 other events, 155.1 us)
Sparse Core Ops, SparseCore 0:
  272.3 86.9 all-gather.30
  631.1 83.0 all-gather.32
  987.4 83.0 all-gather.34
  1356.1 83.7 all-gather.36
  1719.7 83.0 all-gather.38
  2075.7 309.1 all-reduce.8
  2386.8 33.3 all-gather.40
where the time goes:
time: 2450 us; the launch traced here: 2440 us
  blocking collectives  1560 us (64%)
  waiting for transfers between devices  709 us (29%)
  local copies, waits for them, and re-layouts  77.5 us (3%)
  matrix products  36.8 us (2%)
  other arithmetic  29.2 us (1%)
    all_gather x24, blocking collectives, halo(): lax.all_gather(shortened(edge_strips(field)), 'tile', axis=0, tiled=True)  1560 us
    all_gather x6, waiting for transfers between devices, pull(): everyone = lax.all_gather(lines, 'face', axis=0, tiled=True)  404 us
    psum x1, waiting for transfers between devices, summed(): return lax.psum(grad, ('face', 'tile'))  304 us
  transfers between devices with their start and end apart: 7, of which 7 were waited for; matrix products, arithmetic and copies ran while one was open for 2% of the time, Pallas kernels for 0%

commit v1 on v0

v1 whole, which is shorter than its diff:
```python
import math

import jax
import jax.numpy as jnp
import numpy as np
from jax import lax
from jax.experimental import pallas as pl
from jax.experimental.pallas import tpu as pltpu
from jax.sharding import PartitionSpec as P

FACES = 12
TGR = 4
TGC = 8
TH = 24
TW = 12
C = 128
NS = 96
PITCH = 16
CELLS = TH * PITCH
GROUPS = 6
OWNERS = 24
CHUNK = 9 * C // OWNERS
KZ = 512
ROWS = 26 * PITCH
MESH = pl.DeviceIdType.MESH
BF = jnp.bfloat16
F32 = jnp.float32
TAP_TABLE = ((0, 1, 2), (6, 7, 8), (0, 3, 6), (2, 5, 8))


def spread_matrix():
    out = np.zeros((3, ROWS, KZ), np.float32)
    top, bottom, left, right = CELLS, CELLS + 16, CELLS + 32, CELLS + 64
    for dx in range(3):
        for yy in range(26):
            for x in range(TW):
                y, xx = yy - 1, x + dx - 1
                row = out[dx, yy * PITCH + x]
                inside_y, inside_x = 0 <= y < TH, 0 <= xx < TW
                if inside_y and inside_x:
                    row[y * PITCH + xx] = 1
                if y == -1:
                    row[top + xx + 1] = 1
                if y == TH:
                    row[bottom + xx + 1] = 1
                if not inside_x:
                    side = left if xx < 0 else right
                    row[side + (y + 1 if y < TW else 16 + y - TW + 1)] = 1
    return out.reshape(3 * ROWS, KZ)


def gelu_parts(x):
    c = math.sqrt(2.0 / math.pi)
    sq = x * x
    t = jnp.tanh(c * x * (1.0 + 0.044715 * sq))
    half = 0.5 * (1.0 + t)
    slope = half + 0.5 * x * (1.0 - t * t) * (c * (1.0 + 3.0 * 0.044715 * sq))
    return x * half, slope


def kernel(
    nbr, trn, act, cot, w1, w2, w3, spread,
    gin, grads,
    sel, z, xf, xb, slope, up, wst, wbk, sg, line,
    s1, nb, c1, s2, d2, gb, a1, pb, a2, gf,
    s1sem, nsem, csem, s2sem, d2sem, arsem_s, arsem_r,
):
    k = lax.axis_index("face")
    t = lax.axis_index("tile")
    row = t // TGC
    col = t % TGC
    active = k < GROUPS
    owner = t < OWNERS
    is_coll = (row >= 1) & (row <= 2) & (col >= 2) & (col <= 5)
    unit = (col - 2) * 2 + (row - 1)

    def collector(w):
        return (1 + w % 2) * TGC + 2 + w // 2

    def send(src, dst, ssem, rsem, dev):
        pltpu.make_async_remote_copy(
            src_ref=src, dst_ref=dst, send_sem=ssem, recv_sem=rsem, device_id=dev, device_id_type=MESH
        ).start()

    def await_bytes(ref, sem):
        pltpu.make_async_copy(ref, ref, sem).wait()

    slots = []
    for e in (0, 1):
        for i in range(3):
            slots.append((e, (col + 7 + i) % 8, False))
        for i in range(3):
            slots.append((e, (14 - col + i) % 8, True))
    for e in (2, 3):
        for i in range(4):
            slots.append((e, (2 * row + 7 + i) % 8, False))
        for i in range(4):
            slots.append((e, (13 - 2 * row + i) % 8, True))

    def build_sel():
        j = lax.broadcasted_iota(jnp.int32, (16, CELLS), 0)
        cell = lax.broadcasted_iota(jnp.int32, (16, CELLS), 1)
        for n, (e, w, rev) in enumerate(slots):
            pos = (96 - 12 * w) - j if rev else (12 * w - 1) + j
            local = pos - (12 * col if e < 2 else 24 * row)
            size = TW if e < 2 else TH
            base = (0, (TH - 1) * PITCH, 0, TW - 1)[e]
            stride = 1 if e < 2 else PITCH
            ok = (local >= 0) & (local < size) & (j < 14) & (cell == base + local * stride)
            sel[n * 16 : n * 16 + 16, :] = jnp.where(ok, 1.0, 0.0).astype(BF)

    def exchange_send(x):
        for f in range(2):
            cut = jnp.dot(sel[...], z[f, :CELLS], preferred_element_type=F32)
            s1[x, :, f] = cut.astype(BF).reshape(28, 16, C)

        @pl.when(row == 0)
        def _():
            for i in range(6):
                send(s1.at[x, i], c1.at[x, i], s1sem.at[x, 0], csem.at[x], (k, collector(slots[i][1])))

        @pl.when(row == TGR - 1)
        def _():
            for i in range(6):
                send(s1.at[x, 6 + i], c1.at[x, 6 + i], s1sem.at[x, 1], csem.at[x], (k, collector(slots[6 + i][1])))

        for e, edge in ((2, 0), (3, TGC - 1)):
            @pl.when(col == edge)
            def _():
                base = 12 + 8 * (e - 2)
                for i in range(8):
                    dst = 12 + 4 * (e - 2) + i // 2
                    send(s1.at[x, base + i], c1.at[x, dst], s1sem.at[x, e], csem.at[x], (k, collector(slots[base + i][1])))

        @pl.when(row > 0)
        def _():
            for i in range(3):
                send(s1.at[x, i], nb.at[x, 3 + i], s1sem.at[x, 0], nsem.at[x, 1], (k, (row - 1) * TGC + slots[i][1]))

        @pl.when(row < TGR - 1)
        def _():
            for i in range(3):
                send(s1.at[x, 6 + i], nb.at[x, i], s1sem.at[x, 1], nsem.at[x, 0], (k, (row + 1) * TGC + slots[i][1]))

        @pl.when(col > 0)
        def _():
            send(s1.at[x, 13:15], nb.at[x, 8:10], s1sem.at[x, 2], nsem.at[x, 3], (k, t - 1))

        @pl.when(col < TGC - 1)
        def _():
            send(s1.at[x, 21:23], nb.at[x, 6:8], s1sem.at[x, 3], nsem.at[x, 2], (k, t + 1))

    def sent(x):
        for e, edge in ((0, row == 0), (1, row == TGR - 1)):
            @pl.when(edge)
            def _():
                await_bytes(s1.at[x, 6 * e : 6 * e + 6], s1sem.at[x, e])

            @pl.when(jnp.logical_not(edge))
            def _():
                await_bytes(s1.at[x, 6 * e : 6 * e + 3], s1sem.at[x, e])

        for e, edge in ((2, col == 0), (3, col == TGC - 1)):
            base = 12 + 8 * (e - 2)

            @pl.when(edge)
            def _():
                await_bytes(s1.at[x, base : base + 8], s1sem.at[x, e])

            @pl.when(jnp.logical_not(edge))
            def _():
                await_bytes(s1.at[x, base : base + 2], s1sem.at[x, e])

        @pl.when(is_coll)
        def _():
            await_bytes(s2.at[x], s2sem.at[x])

    def collect(x):
        @pl.when(is_coll)
        def _():
            await_bytes(c1.at[x], csem.at[x])
            for e in range(4):
                for rev in range(2):
                    if e < 2:
                        first, count = 6 * e + 3 * rev, 3
                    else:
                        first, count = 12 + 4 * (e - 2) + 2 * rev, 2
                    total = c1[x, first].astype(F32)
                    for n in range(1, count):
                        total = total + c1[x, first + n].astype(F32)
                    line[2 * e + rev] = total.astype(BF)

            for g in range(GROUPS):
                for e in range(4):
                    for fl in range(2):
                        f = 2 * g + fl
                        code = trn[f, e]
                        s2[x, g, e, fl] = line[(code % 4) * 2 + code // 4, nbr[f, e] % 2]
                    tile = (unit, 24 + unit, (unit // 2) * TGC, (unit // 2) * TGC + TGC - 1)[e]
                    slot = 0 if e < 2 else 1 + unit % 2
                    send(s2.at[x, g, e], d2.at[x, slot, k], s2sem.at[x], d2sem.at[x, 0 if e < 2 else 1], (g, tile))

    def arrived(x, slot, f, e):
        group = nbr[jnp.minimum(2 * k + f, FACES - 1), e] // 2
        out = d2[x, slot, 0, f]
        for g in range(1, GROUPS):
            out = jnp.where(group == g, d2[x, slot, g, f], out)
        return out

    def halo_local(x):
        def summed(first, at):
            for f in range(2):
                z[f, at : at + 16] = (
                    nb[x, first, f].astype(F32) + nb[x, first + 1, f].astype(F32) + nb[x, first + 2, f].astype(F32)
                ).astype(BF)

        def blank(at, size):
            for f in range(2):
                z[f, at : at + size] = jnp.zeros((size, C), BF)

        for side, inner in ((0, row > 0), (1, row < TGR - 1)):
            @pl.when(inner)
            def _():
                await_bytes(nb.at[x, 3 * side : 3 * side + 3], nsem.at[x, side])
                summed(3 * side, CELLS + 16 * side)

            @pl.when(jnp.logical_not(inner))
            def _():
                blank(CELLS + 16 * side, 16)

        for side, inner in ((0, col > 0), (1, col < TGC - 1)):
            at = CELLS + 32 + 32 * side

            @pl.when(inner)
            def _():
                await_bytes(nb.at[x, 6 + 2 * side : 8 + 2 * side], nsem.at[x, 2 + side])
                for f in range(2):
                    for h in range(2):
                        z[f, at + 16 * h : at + 16 * h + 16] = nb[x, 6 + 2 * side + h, f]

            @pl.when(jnp.logical_not(inner))
            def _():
                blank(at, 32)

    def halo_cross(x):
        for e, edge in ((0, row == 0), (1, row == TGR - 1)):
            @pl.when(edge)
            def _():
                await_bytes(d2.at[x, 0], d2sem.at[x, 0])
                for f in range(2):
                    z[f, CELLS + 16 * e : CELLS + 16 * e + 16] = arrived(x, 0, f, e)

        for e, edge in ((2, col == 0), (3, col == TGC - 1)):
            @pl.when(edge)
            def _():
                await_bytes(d2.at[x, 1:3], d2sem.at[x, 1])
                at = CELLS + 32 + 32 * (e - 2)
                for f in range(2):
                    for h in range(2):
                        z[f, at + 16 * h : at + 16 * h + 16] = arrived(x, 1 + h, f, e)

    def widen(f, put):
        for dx in range(3):
            part = jnp.dot(spread[dx * ROWS : (dx + 1) * ROWS, :], z[f], preferred_element_type=F32)
            put(dx, part.astype(BF))

    def conv(x3, w3):
        total = None
        for dy in range(3):
            part = jnp.dot(
                x3[dy * PITCH : dy * PITCH + CELLS, :], w3[dy * 3 * C : (dy + 1) * 3 * C, :],
                preferred_element_type=F32,
            )
            total = part if total is None else total + part
        return total

    def correct(x, l):
        def taps(f, e):
            code = trn[jnp.minimum(2 * k + f, 11), e]
            other, rev = code % 4, code // 4
            first = jnp.where(other == 1, 6, jnp.where(other == 3, 2, 0))
            step = jnp.where(other < 2, 1, 3)
            out = []
            for s in range(3):
                order = jnp.where(rev == 1, 2 - s, s)
                tap = first + step * order
                out.append(wbk[l, tap])
            return out

        def product(windows, weights):
            total = None
            for n, win in enumerate(windows):
                sg[n, 0:16] = win.astype(F32)
            for s in range(3):
                pieces = [sg[n, 2 - s : 18 - s].astype(BF) for n in range(len(windows))]
                lhs = pieces[0] if len(pieces) == 1 else jnp.concatenate(pieces, axis=0)
                part = jnp.dot(lhs, weights[s], preferred_element_type=F32)
                total = part if total is None else total + part
            return total

        for e, edge in ((0, row == 0), (1, row == TGR - 1)):
            @pl.when(edge)
            def _():
                await_bytes(d2.at[x, 0], d2sem.at[x, 0])
                at = 0 if e == 0 else CELLS - PITCH
                for f in range(2):
                    more = product([arrived(x, 0, f, e)], taps(f, e))
                    up[f, at : at + 16] = up[f, at : at + 16] + more

        for e, edge in ((2, col == 0), (3, col == TGC - 1)):
            @pl.when(edge)
            def _():
                await_bytes(d2.at[x, 1:3], d2sem.at[x, 1])
                at = 0 if e == 2 else TW - 1
                for f in range(2):
                    more = product([arrived(x, 1, f, e), arrived(x, 2, f, e)], taps(f, e))
                    for h in range(2):
                        where = pl.ds(h * TW * PITCH + at, TW, stride=PITCH)
                        up[f, where, :] = up[f, where, :] + more[16 * h : 16 * h + TW]

    def reduce_send(l):
        @pl.loop(1, 32)
        def _(i):
            dst = (t + i) % 32

            @pl.when(dst < OWNERS)
            def _():
                send(
                    gb.at[l, pl.ds(dst * CHUNK, CHUNK)], a1.at[l, 31 - i],
                    arsem_s.at[l, 0], arsem_r.at[l, 0], (k, dst),
                )

    def reduce_mid(l):
        @pl.when(owner)
        def _():
            await_bytes(a1.at[l], arsem_r.at[l, 0])
            total = gb[l, pl.ds(t * CHUNK, CHUNK)].astype(F32)
            for s in range(31):
                total = total + a1[l, s].astype(F32)
            pb[l] = total.astype(BF)
            a2[l, k] = pb[l]
            for i in range(1, 8):
                send(pb.at[l], a2.at[l, k], arsem_s.at[l, 1], arsem_r.at[l, 1], ((k + i) % 8, t))

    def reduce_last(l):
        @pl.when(owner)
        def _():
            @pl.when(active)
            def _():
                await_bytes(a2.at[l, 0:5], arsem_r.at[l, 1])

            @pl.when(jnp.logical_not(active))
            def _():
                await_bytes(a2.at[l], arsem_r.at[l, 1])

            total = a2[l, 0].astype(F32)
            for s in range(1, GROUPS):
                total = total + a2[l, s].astype(F32)
            mine = pl.ds(t * CHUNK, CHUNK)
            gf[l, mine] = total.astype(BF)

            @pl.loop(1, 32)
            def _(i):
                send(gf.at[l, mine], gf.at[l, mine], arsem_s.at[l, 2], arsem_r.at[l, 2], (k, (t + i) % 32))

    def reduce_drain(l):
        @pl.when(owner)
        def _():
            await_bytes(gf.at[l, 0 : (OWNERS - 1) * CHUNK], arsem_r.at[l, 2])
            await_bytes(a1.at[l], arsem_s.at[l, 2])

            @pl.when(active)
            def _():
                await_bytes(gb.at[l, 0 : (OWNERS - 1) * CHUNK], arsem_s.at[l, 0])
                await_bytes(a1.at[l, 0:7], arsem_s.at[l, 1])

        @pl.when(jnp.logical_not(owner))
        def _():
            await_bytes(gf.at[l], arsem_r.at[l, 2])

            @pl.when(active)
            def _():
                await_bytes(gb.at[l], arsem_s.at[l, 0])

    @pl.when(active)
    def _():
        build_sel()
        for f in range(2):
            z[f, :CELLS] = act[f]
            z[f, CELLS:] = jnp.zeros((KZ - CELLS, C), BF)
        sg[...] = jnp.zeros_like(sg)
        exchange_send(0)
        for l, w in enumerate((w1, w2, w3)):
            for tap in range(9):
                wst[l, tap * C : (tap + 1) * C] = w[tap]
                wbk[l, tap] = w[tap].astype(F32).T.astype(BF)
        for f in range(2):
            up[f] = cot[f].astype(F32)

        @pl.loop(0, 3)
        def _(l):
            collect(l)
            halo_local(l)
            halo_cross(l)
            for f in range(2):
                def put(dx, part):
                    xf[l, f, :, dx * C : (dx + 1) * C] = part

                widen(f, put)
                pre = conv(xf[l, f], wst[l])
                hidden, tilt = gelu_parts(pre)
                slope[l, f] = tilt
                z[f, :CELLS] = hidden.astype(BF)

            @pl.when(l < 2)
            def _():
                exchange_send(l + 1)

        @pl.loop(0, 3)
        def _(i):
            l = 2 - i
            x = 3 + i
            for f in range(2):
                z[f, :CELLS] = (up[f] * slope[l, f]).astype(BF)
            exchange_send(x)
            collect(x)
            for dy in range(3):
                total = None
                for f in range(2):
                    part = lax.dot_general(
                        xf[l, f, dy * PITCH : dy * PITCH + CELLS, :], z[f, :CELLS],
                        (((0,), (0,)), ((), ())), preferred_element_type=F32,
                    )
                    total = part if total is None else total + part
                gb[l, dy * 3 * C : (dy + 1) * 3 * C] = total.astype(BF)
            reduce_send(l)

            @pl.when(i > 0)
            def _():
                reduce_mid(l + 1)

            @pl.when(i > 1)
            def _():
                reduce_last(l + 2)

            halo_local(x)
            for f in range(2):
                def put(dx, part):
                    xb[f, :, dx * C : (dx + 1) * C] = part

                widen(f, put)
                total = None
                for dy in range(3):
                    for dx in range(3):
                        part = jnp.dot(
                            xb[f, dy * PITCH : dy * PITCH + CELLS, dx * C : (dx + 1) * C], wbk[l, 8 - 3 * dy - dx],
                            preferred_element_type=F32,
                        )
                        total = part if total is None else total + part
                up[f] = total
            correct(x, l)

        for f in range(2):
            gin[f] = up[f].astype(BF)
        reduce_mid(0)
        reduce_last(1)
        reduce_last(0)

        @pl.loop(0, 6)
        def _(x):
            sent(x)

    @pl.when(jnp.logical_not(active))
    def _():
        gin[...] = jnp.zeros_like(gin)
        reduce_last(2)
        reduce_last(1)
        reduce_last(0)

    for l in range(3):
        reduce_drain(l)
        grads[l] = gf[l]


def shards(activation, cotangent, weight_one, weight_two, weight_three, neighbor, turn):
    def padded(field):
        return jnp.pad(field[:, 0], ((0, 0), (0, 0), (0, PITCH - TW), (0, 0))).reshape(2, CELLS, C)

    vmem = pl.BlockSpec(memory_space=pltpu.VMEM)
    smem = pl.BlockSpec(memory_space=pltpu.SMEM)
    dma = pltpu.SemaphoreType.DMA
    gin, grads = pl.pallas_call(
        kernel,
        out_shape=(
            jax.ShapeDtypeStruct((2, CELLS, C), BF),
            jax.ShapeDtypeStruct((3, 9 * C, C), BF),
        ),
        in_specs=[smem, smem] + [vmem] * 6,
        out_specs=(vmem, vmem),
        scratch_shapes=[
            pltpu.VMEM((28 * 16, CELLS), BF),
            pltpu.VMEM((2, KZ, C), BF),
            pltpu.VMEM((3, 2, ROWS, 3 * C), BF),
            pltpu.VMEM((2, ROWS, 3 * C), BF),
            pltpu.VMEM((3, 2, CELLS, C), F32),
            pltpu.VMEM((2, CELLS, C), F32),
            pltpu.VMEM((3, 9 * C, C), BF),
            pltpu.VMEM((3, 9, C, C), BF),
            pltpu.VMEM((2, 24, C), F32),
            pltpu.VMEM((8, 2, 16, C), BF),
            pltpu.VMEM((6, 28, 2, 16, C), BF),
            pltpu.VMEM((6, 10, 2, 16, C), BF),
            pltpu.VMEM((6, 20, 2, 16, C), BF),
            pltpu.VMEM((6, GROUPS, 4, 2, 16, C), BF),
            pltpu.VMEM((6, 3, GROUPS, 2, 16, C), BF),
            pltpu.VMEM((3, 9 * C, C), BF),
            pltpu.VMEM((3, 31, CHUNK, C), BF),
            pltpu.VMEM((3, CHUNK, C), BF),
            pltpu.VMEM((3, GROUPS, CHUNK, C), BF),
            pltpu.VMEM((3, 9 * C, C), BF),
            dma((6, 4)),
            dma((6, 4)),
            dma((6,)),
            dma((6,)),
            dma((6, 2)),
            dma((3, 3)),
            dma((3, 3)),
        ],
        compiler_params=pltpu.CompilerParams(
            has_side_effects=True, vmem_limit_bytes=48 * 1024 * 1024
        ),
        name="glued_convolutions",
    )(
        neighbor, turn, padded(activation), padded(cotangent), weight_one, weight_two, weight_three,
        jnp.asarray(spread_matrix(), BF),
    )
    grad_input = gin.reshape(2, 1, TH, PITCH, C)[:, :, :, :TW]
    scaled = grads.reshape(3, 9, C, C).astype(F32) * (1.0 / math.sqrt(FACES * NS * NS))
    return grad_input, scaled[0], scaled[1], scaled[2]


def solution(mesh):
    field = P("face", "tile", None, None, None)
    return jax.shard_map(
        shards,
        mesh=mesh,
        in_specs=(field, field, P(), P(), P(), P(), P()),
        out_specs=(field, P(), P(), P()),
        check_vma=False,
    )
```

time: 2450 us -> 139 us (0.06)
  blocking collectives: 1560 us -> 0 us
  waiting for transfers between devices: 709 us -> 0 us
  Pallas kernels: 0 us -> 129 us
  local copies, waits for them, and re-layouts: 77.5 us -> 8.44 us
  matrix products: 36.8 us -> 0 us
  other arithmetic: 29.2 us -> 0.14 us
    all_gather x24 -> x0, blocking collectives: 1560 us -> none  [halo(): lax.all_gather(shortened(edge_strips(field)), 'tile', axis=0, tiled=True)]
    all_gather x6 -> x0, waiting for transfers between devices: 404 us -> none  [pull(): everyone = lax.all_gather(lines, 'face', axis=0, tiled=True)]
    psum x1 -> x0, waiting for transfers between devices: 304 us -> none  [summed(): return lax.psum(grad, ('face', 'tile'))]
    pallas_call x0 -> x1, Pallas kernels: none -> 129 us  [shards(): pl.pallas_call(kernel, out_shape=(jax.ShapeDtypeStruct((2, CELLS, C), BF)...]
    dot_general x93 -> x0, matrix products: 36.8 us -> none  [the longest x27 12.4 us: weight_grad(): lax.dot_general(window, flat_grad, (((0,), (0,)), ((), ())), preferred_el...]
  transfers between devices with their start and end apart: 7 -> 0, of which waited for: 7 -> 0; matrix products, arithmetic and copies ran while one was open for 2% -> 0% of each run, Pallas kernels for 0% -> 0%
where the time goes in v1:
time: 139 us; the launch traced here: 138 us
  Pallas kernels  129 us (93%)
  local copies, waits for them, and re-layouts  8.44 us (6%)
    pallas_call x1, Pallas kernels, shards(): pl.pallas_call(kernel, out_shape=(jax.ShapeDtypeStruct((2, CELLS, C), BF)...  129 us
    unnamed x13, local copies, waits for them, and re-layouts  7.12 us

profile of v1, /device:TPU:1, one launch (start us, length us, event | category | flops | bytes accessed | tf_op | source)
XLA Modules:
  0.0 138.3 jit_solution(11271003694933308933)
XLA Ops:
  0.6 0.0 copy-start
  0.6 0.9 copy.14.nbr
  1.5 0.8 copy.15.trn
  2.3 0.9 copy.18
  3.3 0.9 copy.19
  4.3 0.0 copy-done
  4.3 0.0 copy-start.1
  4.3 1.0 copy-done.1
  5.3 0.0 copy-start.2
  5.3 1.0 copy-done.2
  6.2 0.0 copy-start.3
  6.2 1.0 copy-done.3
  7.2 129.0 %glued_convolutions.1 = (bf16[2,384,128]{2,1,0:T(8,128)(2,1)S(1)}, bf16[3,1152,128]{2,1,0:T(8,128)(2,1)S(1)}) custom-call(s32[12,4]{1,0:T(8,128)S(1)} %copy.14.nbr, s32[12,4]{1,0:T(8,128)S(1)} %copy.15.trn, bf16[2,384,128]{2,1,0:T(8,128)(2,1)S(1)} %bitcast.9, bf16[2,384,128]{2,1,0:T(8,128)(2,1)S(1)} %bitcast.10, bf16[9,128,128]{2,1,0:T(8,128)(2,1)S(1)} %copy-done.1, ...), custom_call_target="tpu_custom_call" | custom-call | tf_op jit(solution)/shard_map/glued_convolutions/pallas_call | solution.py:492
  136.2 0.7 copy.17
  136.9 0.1 convert_multiply_fusion
  137.0 1.2 fusion
  (2 shorter events, 0.1 us)
Async XLA Ops:
  0.6 3.7 %copy-start = (bf16[1248,512]{1,0:T(8,128)(2,1)S(1)}, bf16[1248,512]{1,0:T(8,128)(2,1)}, u32[]{:S(2)}) copy-start(bf16[1248,512]{1,0:T(8,128)(2,1)} %constant.7.clone.spread) | copy-start | bytes 3833860
  4.3 1.0 copy-start.1
  5.3 1.0 copy-start.2
  6.2 1.0 copy-start.3

commit v2 on v1

v2 whole, which is shorter than its diff:
```python
import math

import jax
import jax.numpy as jnp
import numpy as np
from jax import lax
from jax.experimental import pallas as pl
from jax.experimental.pallas import tpu as pltpu
from jax.sharding import PartitionSpec as P

FACES = 12
TGR = 4
TGC = 8
TH = 24
TW = 12
C = 128
NS = 96
PITCH = 16
CELLS = TH * PITCH
GROUPS = 6
OWNERS = 24
CHUNK = 9 * C // OWNERS
KZ = 512
ROWS = 26 * PITCH
MESH = pl.DeviceIdType.MESH
BF = jnp.bfloat16
F32 = jnp.float32
TAP_TABLE = ((0, 1, 2), (6, 7, 8), (0, 3, 6), (2, 5, 8))


def spread_matrix():
    out = np.zeros((3, ROWS, KZ), np.float32)
    top, bottom, left, right = CELLS, CELLS + 16, CELLS + 32, CELLS + 64
    for dx in range(3):
        for yy in range(26):
            for x in range(TW):
                y, xx = yy - 1, x + dx - 1
                row = out[dx, yy * PITCH + x]
                inside_y, inside_x = 0 <= y < TH, 0 <= xx < TW
                if inside_y and inside_x:
                    row[y * PITCH + xx] = 1
                if y == -1:
                    row[top + xx + 1] = 1
                if y == TH:
                    row[bottom + xx + 1] = 1
                if not inside_x:
                    side = left if xx < 0 else right
                    row[side + (y + 1 if y < TW else 16 + y - TW + 1)] = 1
    return out.reshape(3 * ROWS, KZ)


def gelu_parts(x):
    c = math.sqrt(2.0 / math.pi)
    sq = x * x
    t = jnp.tanh(c * x * (1.0 + 0.044715 * sq))
    half = 0.5 * (1.0 + t)
    slope = half + 0.5 * x * (1.0 - t * t) * (c * (1.0 + 3.0 * 0.044715 * sq))
    return x * half, slope


def kernel(
    nbr_h, trn_h, act_h, cot_h, w1_h, w2_h, w3_h, spread_h,
    gin, grads,
    nbr, trn, act, cot, spread, sel, z, xf, xb, slope, up, wst, wbk, sg, line,
    s1, nb, cr, cc, s2r, s2c, d2r, d2c, gb, a1, pb, a2, gf,
    insem, s1sem, nsem, crsem, ccsem, s2sem, d2sem, arsem_s, arsem_r,
):
    k = lax.axis_index("face")
    t = lax.axis_index("tile")
    row = t // TGC
    col = t % TGC
    active = k < GROUPS
    owner = t < OWNERS
    edges = (row == 0, row == TGR - 1, col == 0, col == TGC - 1)

    barrier = pltpu.get_barrier_semaphore()
    for i in range(1, 8):
        pl.semaphore_signal(barrier, inc=1, device_id=((k + i) % 8, t), device_id_type=MESH)

    @pl.loop(1, 32)
    def _(i):
        pl.semaphore_signal(barrier, inc=1, device_id=(k, (t + i) % 32), device_id_type=MESH)

    def send(src, dst, ssem, rsem, dev):
        pltpu.make_async_remote_copy(
            src_ref=src, dst_ref=dst, send_sem=ssem, recv_sem=rsem, device_id=dev, device_id_type=MESH
        ).start()

    def await_bytes(ref, sem):
        pltpu.make_async_copy(ref, ref, sem).wait()

    def mine(f):
        return jnp.minimum(2 * k + f, FACES - 1)

    slots = []
    for e in (0, 1):
        for i in range(3):
            slots.append((e, (col + 7 + i) % 8, False))
        for i in range(3):
            slots.append((e, (14 - col + i) % 8, True))
    for e in (2, 3):
        for i in range(4):
            slots.append((e, (2 * row + 7 + i) % 8, False))
        for i in range(4):
            slots.append((e, (13 - 2 * row + i) % 8, True))

    def build_sel():
        j = lax.broadcasted_iota(jnp.int32, (16, CELLS), 0)
        cell = lax.broadcasted_iota(jnp.int32, (16, CELLS), 1)
        for n, (e, w, rev) in enumerate(slots):
            pos = (96 - 12 * w) - j if rev else (12 * w - 1) + j
            local = pos - (12 * col if e < 2 else 24 * row)
            size = TW if e < 2 else TH
            base = (0, (TH - 1) * PITCH, 0, TW - 1)[e]
            stride = 1 if e < 2 else PITCH
            ok = (local >= 0) & (local < size) & (j < 14) & (cell == base + local * stride)
            sel[n * 16 : n * 16 + 16, :] = jnp.where(ok, 1.0, 0.0).astype(BF)

    def messages(x, e):
        span = 3 if e < 2 else 4
        first = 6 * e if e < 2 else 12 + 8 * (e - 2)
        for o in range(2):
            for i in range(span):
                n = first + span * o + i
                w = slots[n][1]
                h = w % 2
                at = 6 * e + 3 * o + i if e < 2 else 12 + 4 * (e - 2) + 2 * o + i // 2
                for far in range(2):
                    yield None, n, cr.at[x, at], crsem.at[x], 24 * far + w
                for far in range(2):
                    tile = (w // 2) * TGC + (TGC - 1) * far
                    if e >= 2:
                        yield None, n, cc.at[x, h, 8 + 4 * (e - 2) + 2 * o + i // 2], ccsem.at[x], tile
                    elif i == 0:
                        yield h == 1, n, cc.at[x, 1, 4 * e + 2 * o], ccsem.at[x], tile
                    elif i == 1:
                        yield None, n, cc.at[x, h, 4 * e + 2 * o + h], ccsem.at[x], tile
                    else:
                        yield h == 0, n, cc.at[x, 0, 4 * e + 2 * o + 1], ccsem.at[x], tile

    def exchange_send(x, v):
        for f in range(2):
            cut = jnp.dot(sel[...], v[f, :CELLS], preferred_element_type=F32)
            s1[x, :, f] = cut.astype(BF).reshape(28, 16, C)

        for e in range(4):
            @pl.when(edges[e])
            def _():
                for cond, n, dst, sem, tile in messages(x, e):
                    away, home = tile != t, tile == t
                    if cond is not None:
                        away, home = away & cond, home & cond

                    @pl.when(away)
                    def _():
                        send(s1.at[x, n], dst, s1sem.at[x, e], sem, (k, tile))

                    @pl.when(home)
                    def _():
                        pltpu.make_async_copy(s1.at[x, n], dst, sem).start()

        @pl.when(row > 0)
        def _():
            for i in range(3):
                send(s1.at[x, i], nb.at[x, 3 + i], s1sem.at[x, 0], nsem.at[x, 1], (k, (row - 1) * TGC + slots[i][1]))

        @pl.when(row < TGR - 1)
        def _():
            for i in range(3):
                send(s1.at[x, 6 + i], nb.at[x, i], s1sem.at[x, 1], nsem.at[x, 0], (k, (row + 1) * TGC + slots[i][1]))

        @pl.when(col > 0)
        def _():
            send(s1.at[x, 13:15], nb.at[x, 8:10], s1sem.at[x, 2], nsem.at[x, 3], (k, t - 1))

        @pl.when(col < TGC - 1)
        def _():
            send(s1.at[x, 21:23], nb.at[x, 6:8], s1sem.at[x, 3], nsem.at[x, 2], (k, t + 1))

    def sent(x):
        for e in range(4):
            first = 6 * e if e < 2 else 13 + 8 * (e - 2)

            @pl.when(edges[e])
            def _():
                for cond, n, dst, sem, tile in messages(x, e):
                    away = tile != t
                    if cond is not None:
                        away = away & cond

                    @pl.when(away)
                    def _():
                        await_bytes(s1.at[x, n], s1sem.at[x, e])

                if e < 2:
                    await_bytes(s2r.at[x, 0:5], s2sem.at[x, 0])
                else:
                    await_bytes(s2c.at[x, 0:5], s2sem.at[x, 1])

            @pl.when(jnp.logical_not(edges[e]))
            def _():
                await_bytes(s1.at[x, first : first + (3 if e < 2 else 2)], s1sem.at[x, e])

    def collect(x):
        def lines(buf, row_first, row_count, col_first):
            for e in range(4):
                for o in range(2):
                    if e < 2:
                        first, count = row_first(e, o), row_count
                    else:
                        first, count = col_first(e, o), 2
                    total = buf[first].astype(F32)
                    for n in range(1, count):
                        total = total + buf[first + n].astype(F32)
                    line[2 * e + o] = total.astype(BF)

        def pick(face, e):
            code = trn[face, e]
            return line[(code % 4) * 2 + code // 4, nbr[face, e] % 2]

        for e in range(2):
            @pl.when(edges[e])
            def _():
                await_bytes(cr.at[x], crsem.at[x])
                lines(cr.at[x], lambda e, o: 6 * e + 3 * o, 3, lambda e, o: 12 + 4 * (e - 2) + 2 * o)
                for g in range(GROUPS):
                    for f in range(2):
                        s2r[x, g, f] = pick(2 * g + f, e)
                d2r[x, k] = s2r[x, k]
                for i in range(1, GROUPS):
                    g = (k + i) % GROUPS
                    send(s2r.at[x, g], d2r.at[x, k], s2sem.at[x, 0], d2sem.at[x, 0], (g, t))

        for e in range(2, 4):
            @pl.when(edges[e])
            def _():
                await_bytes(cc.at[x], ccsem.at[x])
                for h in range(2):
                    lines(cc.at[x, h], lambda e, o: 4 * e + 2 * o, 2, lambda e, o: 8 + 4 * (e - 2) + 2 * o)
                    for g in range(GROUPS):
                        for f in range(2):
                            s2c[x, g, h, f] = pick(2 * g + f, e)
                d2c[x, k] = s2c[x, k]
                for i in range(1, GROUPS):
                    g = (k + i) % GROUPS
                    send(s2c.at[x, g], d2c.at[x, k], s2sem.at[x, 1], d2sem.at[x, 1], (g, t))

    def arrived(x, e, f, h=0):
        group = nbr[mine(f), e] // 2
        out = None
        for g in range(GROUPS):
            win = d2r[x, g, f] if e < 2 else d2c[x, g, h, f]
            out = win if out is None else jnp.where(group == g, win, out)
        return out

    def halo_local(x, v):
        for side in (0, 1):
            at = CELLS + 16 * side

            @pl.when(jnp.logical_not(edges[side]))
            def _():
                await_bytes(nb.at[x, 3 * side : 3 * side + 3], nsem.at[x, side])
                for f in range(2):
                    total = nb[x, 3 * side, f].astype(F32) + nb[x, 3 * side + 1, f].astype(F32)
                    v[f, at : at + 16] = (total + nb[x, 3 * side + 2, f].astype(F32)).astype(BF)

            @pl.when(edges[side])
            def _():
                for f in range(2):
                    v[f, at : at + 16] = jnp.zeros((16, C), BF)

        for side in (0, 1):
            at = CELLS + 32 + 32 * side

            @pl.when(jnp.logical_not(edges[2 + side]))
            def _():
                await_bytes(nb.at[x, 6 + 2 * side : 8 + 2 * side], nsem.at[x, 2 + side])
                for f in range(2):
                    for h in range(2):
                        v[f, at + 16 * h : at + 16 * h + 16] = nb[x, 6 + 2 * side + h, f]

            @pl.when(edges[2 + side])
            def _():
                for f in range(2):
                    v[f, at : at + 32] = jnp.zeros((32, C), BF)

    def widen(f, v, out):
        for dx in range(3):
            part = jnp.dot(spread[dx * ROWS : (dx + 1) * ROWS, :], v[f], preferred_element_type=F32)
            out[f, :, dx * C : (dx + 1) * C] = part.astype(BF)

    def finish(l):
        v = z.at[l]
        for e in range(4):
            @pl.when(edges[e])
            def _():
                for f in range(2):
                    if e < 2:
                        at = CELLS + 16 * e
                        v[f, at : at + 16] = arrived(l, e, f)
                    else:
                        for h in range(2):
                            at = CELLS + 32 + 32 * (e - 2) + 16 * h
                            v[f, at : at + 16] = arrived(l, e, f, h)

        @pl.when(edges[0] | edges[1] | edges[2] | edges[3])
        def _():
            for f in range(2):
                widen(f, v, xf.at[l])

    def correct(x, weights):
        for e in range(4):
            @pl.when(edges[e])
            def _():
                if e < 2:
                    await_bytes(d2r.at[x, 0:5], d2sem.at[x, 0])
                else:
                    await_bytes(d2c.at[x, 0:5], d2sem.at[x, 1])
                size = 16 if e < 2 else 32
                for f in range(2):
                    sg[0, 0:16] = arrived(x, e, f, 0).astype(F32)
                    if e >= 2:
                        sg[1, 0:16] = arrived(x, e, f, 1).astype(F32)
                        sg[0, 13:26] = sg[1, 1:14]
                    else:
                        sg[0, 16:32] = jnp.zeros((16, C), F32)
                    more = None
                    for s, weight in enumerate(weights(f, e)):
                        part = jnp.dot(sg[0, s : s + size].astype(BF), weight, preferred_element_type=F32)
                        more = part if more is None else more + part
                    if e < 2:
                        at = 0 if e == 0 else CELLS - PITCH
                        up[f, at : at + 16] = up[f, at : at + 16] + more
                    else:
                        where = pl.ds(0 if e == 2 else TW - 1, TH, stride=PITCH)
                        up[f, where, :] = up[f, where, :] + more[0:TH]

    def forward_taps(l):
        return lambda f, e: [wst[l, tap] for tap in TAP_TABLE[e]]

    def backward_taps(l):
        def weights(f, e):
            code = trn[mine(f), e]
            other, rev = code % 4, code // 4
            first = jnp.where(other == 1, 6, jnp.where(other == 3, 2, 0))
            step = jnp.where(other < 2, 1, 3)
            out = []
            for s in range(3):
                order = jnp.where(rev == 1, s, 2 - s)
                out.append(wbk[l, first + step * order])
            return out

        return weights

    def reduce_send(l):
        @pl.loop(1, 32)
        def _(i):
            dst = (t + i) % 32

            @pl.when(dst < OWNERS)
            def _():
                send(
                    gb.at[l, pl.ds(dst * CHUNK, CHUNK)], a1.at[l, 31 - i],
                    arsem_s.at[l, 0], arsem_r.at[l, 0], (k, dst),
                )

    def reduce_mid(l):
        @pl.when(owner)
        def _():
            await_bytes(a1.at[l], arsem_r.at[l, 0])
            total = gb[l, pl.ds(t * CHUNK, CHUNK)].astype(F32)
            for s in range(31):
                total = total + a1[l, s].astype(F32)
            pb[l] = total.astype(BF)
            a2[l, k] = pb[l]
            for i in range(1, 8):
                send(pb.at[l], a2.at[l, k], arsem_s.at[l, 1], arsem_r.at[l, 1], ((k + i) % 8, t))

    def reduce_last(l):
        @pl.when(owner)
        def _():
            @pl.when(active)
            def _():
                await_bytes(a2.at[l, 0:5], arsem_r.at[l, 1])

            @pl.when(jnp.logical_not(active))
            def _():
                await_bytes(a2.at[l], arsem_r.at[l, 1])

            total = a2[l, 0].astype(F32)
            for s in range(1, GROUPS):
                total = total + a2[l, s].astype(F32)
            here = pl.ds(t * CHUNK, CHUNK)
            gf[l, here] = total.astype(BF)

            @pl.loop(1, 32)
            def _(i):
                send(gf.at[l, here], gf.at[l, here], arsem_s.at[l, 2], arsem_r.at[l, 2], (k, (t + i) % 32))

    def reduce_drain(l):
        @pl.when(owner)
        def _():
            await_bytes(gf.at[l, 0 : (OWNERS - 1) * CHUNK], arsem_r.at[l, 2])
            await_bytes(a1.at[l], arsem_s.at[l, 2])

            @pl.when(active)
            def _():
                await_bytes(gb.at[l, 0 : (OWNERS - 1) * CHUNK], arsem_s.at[l, 0])
                await_bytes(a1.at[l, 0:7], arsem_s.at[l, 1])

        @pl.when(jnp.logical_not(owner))
        def _():
            await_bytes(gf.at[l], arsem_r.at[l, 2])

            @pl.when(active)
            def _():
                await_bytes(gb.at[l], arsem_s.at[l, 0])

    fetches = [
        pltpu.make_async_copy(src, dst, insem.at[n])
        for n, (src, dst) in enumerate((
            (act_h.at[:, 0], act), (w1_h, wst.at[0]), (spread_h, spread), (nbr_h, nbr), (trn_h, trn),
            (w2_h, wst.at[1]), (w3_h, wst.at[2]), (cot_h.at[:, 0], cot),
        ))
    ]

    @pl.when(active)
    def _():
        for fetch in fetches:
            fetch.start()
        build_sel()
        z[...] = jnp.zeros_like(z)
        up[...] = jnp.zeros_like(up)
        sg[...] = jnp.zeros_like(sg)
        fetches[0].wait()
        for f in range(2):
            for y in range(TH):
                z[0, f, y * PITCH : y * PITCH + TW] = act[f, y]

    pl.semaphore_wait(barrier, 38)

    @pl.when(active)
    def _():
        @pl.loop(0, 3)
        def _(l):
            exchange_send(l, z.at[l])

            @pl.when(l == 0)
            def _():
                for fetch in fetches[1:]:
                    fetch.wait()

            @pl.when(l > 0)
            def _():
                finish(l - 1)

            collect(l)
            halo_local(l, z.at[l])
            for f in range(2):
                widen(f, z.at[l], xf.at[l])
                total = None
                for dy in range(3):
                    part = jnp.dot(
                        xf[l, f, dy * PITCH : dy * PITCH + CELLS, :],
                        wst[l, 3 * dy : 3 * dy + 3].reshape(3 * C, C), preferred_element_type=F32,
                    )
                    total = part if total is None else total + part
                up[f] = total
            correct(l, forward_taps(l))
            for f in range(2):
                hidden, tilt = gelu_parts(up[f])
                slope[l, f] = tilt
                z[l + 1, f, :CELLS] = hidden.astype(BF)

        for f in range(2):
            up[f] = jnp.zeros((CELLS, C), F32)
            for y in range(TH):
                up[f, y * PITCH : y * PITCH + TW] = cot[f, y].astype(F32)

        @pl.loop(0, 3)
        def _(i):
            l = 2 - i
            x = 3 + i
            d = z.at[3]
            for f in range(2):
                d[f, :CELLS] = (up[f] * slope[l, f]).astype(BF)
            exchange_send(x, d)

            @pl.when(i == 0)
            def _():
                finish(2)
                for n in range(3):
                    for tap in range(9):
                        wbk[n, tap] = wst[n, tap].astype(F32).T.astype(BF)

            collect(x)
            for dy in range(3):
                total = None
                for f in range(2):
                    part = lax.dot_general(
                        xf[l, f, dy * PITCH : dy * PITCH + CELLS, :], d[f, :CELLS],
                        (((0,), (0,)), ((), ())), preferred_element_type=F32,
                    )
                    total = part if total is None else total + part
                gb[l, dy * 3 * C : (dy + 1) * 3 * C] = total.astype(BF)
            reduce_send(l)

            @pl.when(i > 0)
            def _():
                reduce_mid(l + 1)

            @pl.when(i > 1)
            def _():
                reduce_last(l + 2)

            halo_local(x, d)
            for f in range(2):
                widen(f, d, xb)
                total = None
                for dy in range(3):
                    for dx in range(3):
                        part = jnp.dot(
                            xb[f, dy * PITCH : dy * PITCH + CELLS, dx * C : (dx + 1) * C], wbk[l, 8 - 3 * dy - dx],
                            preferred_element_type=F32,
                        )
                        total = part if total is None else total + part
                up[f] = total

            @pl.when(i == 2)
            def _():
                reduce_mid(l)

            correct(x, backward_taps(l))

        for f in range(2):
            gin[f] = up[f].astype(BF)
        reduce_last(1)
        reduce_last(0)

        @pl.loop(0, 6)
        def _(x):
            sent(x)

    @pl.when(jnp.logical_not(active))
    def _():
        gin[...] = jnp.zeros_like(gin)
        reduce_last(2)
        reduce_last(1)
        reduce_last(0)

    for l in range(3):
        reduce_drain(l)
        grads[l] = gf[l]


def shards(activation, cotangent, weight_one, weight_two, weight_three, neighbor, turn):
    vmem = pl.BlockSpec(memory_space=pltpu.VMEM)
    hbm = pl.BlockSpec(memory_space=pl.ANY)
    dma = pltpu.SemaphoreType.DMA
    gin, grads = pl.pallas_call(
        kernel,
        out_shape=(
            jax.ShapeDtypeStruct((2, CELLS, C), BF),
            jax.ShapeDtypeStruct((3, 9 * C, C), BF),
        ),
        in_specs=[hbm] * 8,
        out_specs=(vmem, vmem),
        scratch_shapes=[
            pltpu.SMEM((FACES, 4), jnp.int32),
            pltpu.SMEM((FACES, 4), jnp.int32),
            pltpu.VMEM((2, TH, TW, C), BF),
            pltpu.VMEM((2, TH, TW, C), BF),
            pltpu.VMEM((3 * ROWS, KZ), BF),
            pltpu.VMEM((28 * 16, CELLS), BF),
            pltpu.VMEM((4, 2, KZ, C), BF),
            pltpu.VMEM((3, 2, ROWS, 3 * C), BF),
            pltpu.VMEM((2, ROWS, 3 * C), BF),
            pltpu.VMEM((3, 2, CELLS, C), F32),
            pltpu.VMEM((2, CELLS, C), F32),
            pltpu.VMEM((3, 9, C, C), BF),
            pltpu.VMEM((3, 9, C, C), BF),
            pltpu.VMEM((2, 40, C), F32),
            pltpu.VMEM((8, 2, 16, C), BF),
            pltpu.VMEM((6, 28, 2, 16, C), BF),
            pltpu.VMEM((6, 10, 2, 16, C), BF),
            pltpu.VMEM((6, 20, 2, 16, C), BF),
            pltpu.VMEM((6, 2, 16, 2, 16, C), BF),
            pltpu.VMEM((6, GROUPS, 2, 16, C), BF),
            pltpu.VMEM((6, GROUPS, 2, 2, 16, C), BF),
            pltpu.VMEM((6, GROUPS, 2, 16, C), BF),
            pltpu.VMEM((6, GROUPS, 2, 2, 16, C), BF),
            pltpu.VMEM((3, 9 * C, C), BF),
            pltpu.VMEM((3, 31, CHUNK, C), BF),
            pltpu.VMEM((3, CHUNK, C), BF),
            pltpu.VMEM((3, GROUPS, CHUNK, C), BF),
            pltpu.VMEM((3, 9 * C, C), BF),
            dma((8,)),
            dma((6, 4)),
            dma((6, 4)),
            dma((6,)),
            dma((6,)),
            dma((6, 2)),
            dma((6, 2)),
            dma((3, 3)),
            dma((3, 3)),
        ],
        compiler_params=pltpu.CompilerParams(
            collective_id=0, has_side_effects=True, vmem_limit_bytes=48 * 1024 * 1024
        ),
        name="glued_convolutions",
    )(
        neighbor, turn, activation, cotangent, weight_one, weight_two, weight_three,
        jnp.asarray(spread_matrix(), BF),
    )
    grad_input = gin.reshape(2, 1, TH, PITCH, C)[:, :, :, :TW]
    scaled = grads.reshape(3, 9, C, C).astype(F32) * (1.0 / math.sqrt(FACES * NS * NS))
    return grad_input, scaled[0], scaled[1], scaled[2]


def solution(mesh):
    field = P("face", "tile", None, None, None)
    return jax.shard_map(
        shards,
        mesh=mesh,
        in_specs=(field, field, P(), P(), P(), P(), P()),
        out_specs=(field, P(), P(), P()),
        check_vma=False,
    )
```

time: 139 us -> 130 us (0.935)
  Pallas kernels: 129 us -> 119 us
    pallas_call x1, Pallas kernels: 129 us -> 119 us  [shards(): pl.pallas_call(kernel, out_shape=(jax.ShapeDtypeStruct((2, CELLS, C), BF)...]
where the time goes in v2:
time: 130 us; the launch traced here: 129 us
  Pallas kernels  119 us (92%)
  local copies, waits for them, and re-layouts  9.56 us (7%)
    pallas_call x1, Pallas kernels, shards(): pl.pallas_call(kernel, out_shape=(jax.ShapeDtypeStruct((2, CELLS, C), BF)...  119 us
    unnamed x13, local copies, waits for them, and re-layouts  8.31 us

profile of v2, /device:TPU:1, one launch (start us, length us, event | category | flops | bytes accessed | tf_op | source)
XLA Modules:
  0.0 129.2 jit_solution(13969659878685266177)
XLA Ops:
  0.6 0.8 copy.12.nbr_h
  1.4 0.8 copy.13.trn_h
  2.2 0.9 copy.14.act_h
  3.1 0.9 copy.15.cot_h
  4.1 0.0 copy-start
  4.1 1.3 %copy-done = bf16[1248,512]{1,0:T(8,128)(2,1)S(1)} copy-done((bf16[1248,512]{1,0:T(8,128)(2,1)S(1)}, bf16[1248,512]{1,0:T(8,128)(2,1)}, u32[]{:S(2)}) %copy-start) | copy-done | bytes 1277976
  5.4 0.0 copy-start.1
  5.4 1.0 copy-done.1
  6.3 0.0 copy-start.2
  6.3 1.0 copy-done.2
  7.3 0.0 copy-start.3
  7.3 1.0 copy-done.3
  8.3 118.9 %glued_convolutions.1 = (bf16[2,384,128]{2,1,0:T(8,128)(2,1)S(1)}, bf16[3,1152,128]{2,1,0:T(8,128)(2,1)S(1)}) custom-call(s32[12,4]{1,0:T(8,128)S(1)} %copy.12.nbr_h, s32[12,4]{1,0:T(8,128)S(1)} %copy.13.trn_h, bf16[2,1,24,12,128]{4,3,2,1,0:T(8,128)(2,1)S(1)} %copy.14.act_h, bf16[2,1,24,12,128]{4,3,2,1,0:T(8,128)(2,1)S(1)} %copy.15.cot_h, ...), custom_call_target="tpu_custom_call" | custom-call | tf_op jit(solution)/shard_map/glued_convolutions/pallas_call | solution.py:560
  127.2 0.7 copy.17
  127.9 0.1 convert_multiply_fusion
  128.0 1.2 fusion
Async XLA Ops:
  4.1 1.3 %copy-start = (bf16[1248,512]{1,0:T(8,128)(2,1)S(1)}, bf16[1248,512]{1,0:T(8,128)(2,1)}, u32[]{:S(2)}) copy-start(bf16[1248,512]{1,0:T(8,128)(2,1)} %constant.4.clone.spread_h) | copy-start | bytes 3833860
  5.4 1.0 copy-start.1
  6.3 1.0 copy-start.2
  7.3 1.0 copy-start.3

commit v3 on v2

--- a/solution.py
+++ b/solution.py
@@ -61,7 +61,7 @@
 def kernel(
     nbr_h, trn_h, act_h, cot_h, w1_h, w2_h, w3_h, spread_h,
     gin, grads,
-    nbr, trn, act, cot, spread, sel, z, xf, xb, slope, up, wst, wbk, sg, line,
+    nbr, trn, pick_at, act, cot, spread, sel, z, xf, xb, slope, up, wst, wbk, sg, line,
     s1, nb, cr, cc, s2r, s2c, d2r, d2c, gb, a1, pb, a2, gf,
     insem, s1sem, nsem, crsem, ccsem, s2sem, d2sem, arsem_s, arsem_r,
 ):
@@ -72,6 +72,9 @@
     active = k < GROUPS
     owner = t < OWNERS
     edges = (row == 0, row == TGR - 1, col == 0, col == TGC - 1)
+    side = col // 4
+    gathers = (row >= 1) & (row <= 2) & (((col >= 1) & (col <= 2)) | ((col >= 5) & (col <= 6)))
+    served = 2 * (col - 1 + side * (7 - 2 * col)) + row - 1
 
     barrier = pltpu.get_barrier_semaphore()
     for i in range(1, 8):
@@ -80,6 +83,23 @@
     @pl.loop(1, 32)
     def _(i):
         pl.semaphore_signal(barrier, inc=1, device_id=(k, (t + i) % 32), device_id_type=MESH)
+
+    def gatherer(r, far):
+        return (1 + r % 2) * TGC + 1 + r // 2 + far * (5 - 2 * (r // 2))
+
+    glued = active & (edges[2] | edges[3])
+    gathering = active & gathers
+
+    @pl.when(glued)
+    def _():
+        for i in range(1, GROUPS):
+            pl.semaphore_signal(barrier, inc=1, device_id=((k + i) % GROUPS, gatherer(row, side)), device_id_type=MESH)
+
+    @pl.when(gathering)
+    def _():
+        for i in range(1, GROUPS):
+            there = served * TGC + (TGC - 1) * side
+            pl.semaphore_signal(barrier, inc=1, device_id=((k + i) % GROUPS, there), device_id_type=MESH)
 
     def send(src, dst, ssem, rsem, dev):
         pltpu.make_async_remote_copy(
@@ -126,17 +146,17 @@
                 h = w % 2
                 at = 6 * e + 3 * o + i if e < 2 else 12 + 4 * (e - 2) + 2 * o + i // 2
                 for far in range(2):
-                    yield None, n, cr.at[x, at], crsem.at[x], 24 * far + w
+                    yield True, None, n, cr.at[x, at], crsem.at[x], 24 * far + w
                 for far in range(2):
-                    tile = (w // 2) * TGC + (TGC - 1) * far
+                    tile = gatherer(w // 2, far)
                     if e >= 2:
-                        yield None, n, cc.at[x, h, 8 + 4 * (e - 2) + 2 * o + i // 2], ccsem.at[x], tile
+                        yield False, None, n, cc.at[x, h, 8 + 4 * (e - 2) + 2 * o + i // 2], ccsem.at[x], tile
                     elif i == 0:
-                        yield h == 1, n, cc.at[x, 1, 4 * e + 2 * o], ccsem.at[x], tile
+                        yield False, h == 1, n, cc.at[x, 1, 4 * e + 2 * o], ccsem.at[x], tile
                     elif i == 1:
-                        yield None, n, cc.at[x, h, 4 * e + 2 * o + h], ccsem.at[x], tile
+                        yield False, None, n, cc.at[x, h, 4 * e + 2 * o + h], ccsem.at[x], tile
                     else:
-                        yield h == 0, n, cc.at[x, 0, 4 * e + 2 * o + 1], ccsem.at[x], tile
+                        yield False, h == 0, n, cc.at[x, 0, 4 * e + 2 * o + 1], ccsem.at[x], tile
 
     def exchange_send(x, v):
         for f in range(2):
@@ -146,18 +166,21 @@
         for e in range(4):
             @pl.when(edges[e])
             def _():
-                for cond, n, dst, sem, tile in messages(x, e):
-                    away, home = tile != t, tile == t
-                    if cond is not None:
-                        away, home = away & cond, home & cond
-
-                    @pl.when(away)
-                    def _():
+                for stays, cond, n, dst, sem, tile in messages(x, e):
+                    if stays:
+                        @pl.when(tile != t)
+                        def _():
+                            send(s1.at[x, n], dst, s1sem.at[x, e], sem, (k, tile))
+
+                        @pl.when(tile == t)
+                        def _():
+                            pltpu.make_async_copy(s1.at[x, n], dst, sem).start()
+                    elif cond is None:
                         send(s1.at[x, n], dst, s1sem.at[x, e], sem, (k, tile))
-
-                    @pl.when(home)
-                    def _():
-                        pltpu.make_async_copy(s1.at[x, n], dst, sem).start()
+                    else:
+                        @pl.when(cond)
+                        def _():
+                            send(s1.at[x, n], dst, s1sem.at[x, e], sem, (k, tile))
 
         @pl.when(row > 0)
         def _():
@@ -183,23 +206,26 @@
 
             @pl.when(edges[e])
             def _():
-                for cond, n, dst, sem, tile in messages(x, e):
-                    away = tile != t
-                    if cond is not None:
-                        away = away & cond
-
-                    @pl.when(away)
-                    def _():
+                for stays, cond, n, dst, sem, tile in messages(x, e):
+                    if stays:
+                        cond = tile != t
+                    if cond is None:
                         await_bytes(s1.at[x, n], s1sem.at[x, e])
+                    else:
+                        @pl.when(cond)
+                        def _():
+                            await_bytes(s1.at[x, n], s1sem.at[x, e])
 
                 if e < 2:
                     await_bytes(s2r.at[x, 0:5], s2sem.at[x, 0])
-                else:
-                    await_bytes(s2c.at[x, 0:5], s2sem.at[x, 1])
 
             @pl.when(jnp.logical_not(edges[e]))
             def _():
                 await_bytes(s1.at[x, first : first + (3 if e < 2 else 2)], s1sem.at[x, e])
+
+        @pl.when(gathers)
+        def _():
+            await_bytes(s2c.at[x], s2sem.at[x, 1])
 
     def collect(x):
         def lines(buf, row_first, row_count, col_first):
@@ -215,8 +241,8 @@
                     line[2 * e + o] = total.astype(BF)
 
         def pick(face, e):
-            code = trn[face, e]
-            return line[(code % 4) * 2 + code // 4, nbr[face, e] % 2]
+            at = pick_at[face, e]
+            return line[at // 2, at % 2]
 
         for e in range(2):
             @pl.when(edges[e])
@@ -231,19 +257,18 @@
                     g = (k + i) % GROUPS
                     send(s2r.at[x, g], d2r.at[x, k], s2sem.at[x, 0], d2sem.at[x, 0], (g, t))
 
-        for e in range(2, 4):
-            @pl.when(edges[e])
-            def _():
-                await_bytes(cc.at[x], ccsem.at[x])
-                for h in range(2):
-                    lines(cc.at[x, h], lambda e, o: 4 * e + 2 * o, 2, lambda e, o: 8 + 4 * (e - 2) + 2 * o)
-                    for g in range(GROUPS):
-                        for f in range(2):
-                            s2c[x, g, h, f] = pick(2 * g + f, e)
-                d2c[x, k] = s2c[x, k]
-                for i in range(1, GROUPS):
-                    g = (k + i) % GROUPS
-                    send(s2c.at[x, g], d2c.at[x, k], s2sem.at[x, 1], d2sem.at[x, 1], (g, t))
+        @pl.when(gathers)
+        def _():
+            await_bytes(cc.at[x], ccsem.at[x])
+            for h in range(2):
+                lines(cc.at[x, h], lambda e, o: 4 * e + 2 * o, 2, lambda e, o: 8 + 4 * (e - 2) + 2 * o)
+                for g in range(GROUPS):
+                    for f in range(2):
+                        s2c[x, g, h, f] = pick(2 * g + f, 2 + side)
+            for i in range(GROUPS):
+                g = (k + i) % GROUPS
+                there = served * TGC + (TGC - 1) * side
+                send(s2c.at[x, g], d2c.at[x, k], s2sem.at[x, 1], d2sem.at[x, 1], (g, there))
 
     def arrived(x, e, f, h=0):
         group = nbr[mine(f), e] // 2
@@ -315,7 +340,7 @@
                 if e < 2:
                     await_bytes(d2r.at[x, 0:5], d2sem.at[x, 0])
                 else:
-                    await_bytes(d2c.at[x, 0:5], d2sem.at[x, 1])
+                    await_bytes(d2c.at[x], d2sem.at[x, 1])
                 size = 16 if e < 2 else 32
                 for f in range(2):
                     sg[0, 0:16] = arrived(x, e, f, 0).astype(F32)
@@ -437,7 +462,13 @@
             for y in range(TH):
                 z[0, f, y * PITCH : y * PITCH + TW] = act[f, y]
 
-    pl.semaphore_wait(barrier, 38)
+    @pl.when(glued | gathering)
+    def _():
+        pl.semaphore_wait(barrier, 38 + GROUPS - 1)
+
+    @pl.when(jnp.logical_not(glued | gathering))
+    def _():
+        pl.semaphore_wait(barrier, 38)
 
     @pl.when(active)
     def _():
@@ -449,6 +480,10 @@
             def _():
                 for fetch in fetches[1:]:
                     fetch.wait()
+                for face in range(FACES):
+                    for e in range(4):
+                        code = trn[face, e]
+                        pick_at[face, e] = (code % 4) * 4 + (code // 4) * 2 + nbr[face, e] % 2
 
             @pl.when(l > 0)
             def _():
@@ -493,7 +528,6 @@
                     for tap in range(9):
                         wbk[n, tap] = wst[n, tap].astype(F32).T.astype(BF)
 
-            collect(x)
             for dy in range(3):
                 total = None
                 for f in range(2):
@@ -503,7 +537,16 @@
                     )
                     total = part if total is None else total + part
                 gb[l, dy * 3 * C : (dy + 1) * 3 * C] = total.astype(BF)
-            reduce_send(l)
+
+            @pl.when(i == 2)
+            def _():
+                reduce_send(l)
+
+            collect(x)
+
+            @pl.when(i < 2)
+            def _():
+                reduce_send(l)
 
             @pl.when(i > 0)
             def _():
@@ -529,12 +572,12 @@
             @pl.when(i == 2)
             def _():
                 reduce_mid(l)
+                reduce_last(l + 1)
 
             correct(x, backward_taps(l))
 
         for f in range(2):
             gin[f] = up[f].astype(BF)
-        reduce_last(1)
         reduce_last(0)
 
         @pl.loop(0, 6)
@@ -555,7 +598,7 @@
 
 def shards(activation, cotangent, weight_one, weight_two, weight_three, neighbor, turn):
     vmem = pl.BlockSpec(memory_space=pltpu.VMEM)
-    hbm = pl.BlockSpec(memory_space=pl.ANY)
+    hbm = pl.BlockSpec(memory_space=pltpu.HBM)
     dma = pltpu.SemaphoreType.DMA
     gin, grads = pl.pallas_call(
         kernel,
@@ -566,6 +609,7 @@
         in_specs=[hbm] * 8,
         out_specs=(vmem, vmem),
         scratch_shapes=[
+            pltpu.SMEM((FACES, 4), jnp.int32),
             pltpu.SMEM((FACES, 4), jnp.int32),
             pltpu.SMEM((FACES, 4), jnp.int32),
             pltpu.VMEM((2, TH, TW, C), BF),

time: 130 us -> 129 us (level)
  no operation moved by 1% of the time
where the time goes in v3:
time: 129 us
  Pallas kernels  119 us (92%)
  local copies, waits for them, and re-layouts  9.56 us (7%)
    pallas_call x1, Pallas kernels, shards(): pl.pallas_call(kernel, out_shape=(jax.ShapeDtypeStruct((2, CELLS, C), BF)...  119 us
    unnamed x13, local copies, waits for them, and re-layouts  8.31 us

profile of v3, /device:TPU:1, one launch (start us, length us, event | category | flops | bytes accessed | tf_op | source)
XLA Modules:
  0.0 129.0 jit_solution(10258889826885224794)
XLA Ops:
  0.6 0.8 copy.12.nbr_h
  1.4 0.8 copy.13.trn_h
  2.2 0.9 copy.14.act_h
  3.1 0.9 copy.15.cot_h
  4.1 0.0 copy-start
  4.1 1.3 %copy-done = bf16[1248,512]{1,0:T(8,128)(2,1)S(1)} copy-done((bf16[1248,512]{1,0:T(8,128)(2,1)S(1)}, bf16[1248,512]{1,0:T(8,128)(2,1)}, u32[]{:S(2)}) %copy-start) | copy-done | bytes 1277976
  5.4 0.0 copy-start.1
  5.4 1.0 copy-done.1
  6.3 0.0 copy-start.2
  6.3 1.0 copy-done.2
  7.3 0.0 copy-start.3
  7.3 1.0 copy-done.3
  8.3 118.7 %glued_convolutions.1 = (bf16[2,384,128]{2,1,0:T(8,128)(2,1)S(1)}, bf16[3,1152,128]{2,1,0:T(8,128)(2,1)S(1)}) custom-call(s32[12,4]{1,0:T(8,128)S(1)} %copy.12.nbr_h, s32[12,4]{1,0:T(8,128)S(1)} %copy.13.trn_h, bf16[2,1,24,12,128]{4,3,2,1,0:T(8,128)(2,1)S(1)} %copy.14.act_h, bf16[2,1,24,12,128]{4,3,2,1,0:T(8,128)(2,1)S(1)} %copy.15.cot_h, ...), custom_call_target="tpu_custom_call" | custom-call | tf_op jit(solution)/shard_map/glued_convolutions/pallas_call | solution.py:603
  127.0 0.7 copy.17
  127.7 0.1 convert_multiply_fusion
  127.8 1.2 fusion
Async XLA Ops:
  4.1 1.3 %copy-start = (bf16[1248,512]{1,0:T(8,128)(2,1)S(1)}, bf16[1248,512]{1,0:T(8,128)(2,1)}, u32[]{:S(2)}) copy-start(bf16[1248,512]{1,0:T(8,128)(2,1)} %constant.4.clone.spread_h) | copy-start | bytes 3833860
  5.4 1.0 copy-start.1
  6.3 1.0 copy-start.2
  7.3 1.0 copy-start.3

commit v4 on v3

--- a/solution.py
+++ b/solution.py
@@ -11,6 +11,7 @@
 FACES = 12
 TGR = 4
 TGC = 8
+TILES = 32
 TH = 24
 TW = 12
 C = 128
@@ -61,7 +62,7 @@
 def kernel(
     nbr_h, trn_h, act_h, cot_h, w1_h, w2_h, w3_h, spread_h,
     gin, grads,
-    nbr, trn, pick_at, act, cot, spread, sel, z, xf, xb, slope, up, wst, wbk, sg, line,
+    nbr, trn, pick_at, act, cot, spread, order, sel, z, xf, xb, slope, up, wst, wbk, sg, line,
     s1, nb, cr, cc, s2r, s2c, d2r, d2c, gb, a1, pb, a2, gf,
     insem, s1sem, nsem, crsem, ccsem, s2sem, d2sem, arsem_s, arsem_r,
 ):
@@ -72,9 +73,9 @@
     active = k < GROUPS
     owner = t < OWNERS
     edges = (row == 0, row == TGR - 1, col == 0, col == TGC - 1)
-    side = col // 4
-    gathers = (row >= 1) & (row <= 2) & (((col >= 1) & (col <= 2)) | ((col >= 5) & (col <= 6)))
-    served = 2 * (col - 1 + side * (7 - 2 * col)) + row - 1
+    gathers = (row >= 1) & (row <= 2) & ((col == 1) | (col == 6))
+    served = 2 * (row - 1) + (col - 1) // 5
+    lines_up = (edges[0] & (col % 2 == 0)) | (edges[1] & (col % 2 == 1))
 
     barrier = pltpu.get_barrier_semaphore()
     for i in range(1, 8):
@@ -84,22 +85,29 @@
     def _(i):
         pl.semaphore_signal(barrier, inc=1, device_id=(k, (t + i) % 32), device_id_type=MESH)
 
-    def gatherer(r, far):
-        return (1 + r % 2) * TGC + 1 + r // 2 + far * (5 - 2 * (r // 2))
-
-    glued = active & (edges[2] | edges[3])
-    gathering = active & gathers
-
-    @pl.when(glued)
+    def gatherer(r):
+        return (1 + r // 2) * TGC + 1 + 5 * (r % 2)
+
+    def aligner(w):
+        return (w % 2) * (TILES - TGC) + w
+
+    def greet(tile):
+        for i in range(1, GROUPS):
+            pl.semaphore_signal(barrier, inc=1, device_id=((k + i) % GROUPS, tile), device_id_type=MESH)
+
+    for e in range(2):
+        @pl.when(active & edges[e])
+        def _():
+            greet((1 - e) * (TILES - TGC) + col)
+
+    @pl.when(active & (edges[2] | edges[3]))
     def _():
-        for i in range(1, GROUPS):
-            pl.semaphore_signal(barrier, inc=1, device_id=((k + i) % GROUPS, gatherer(row, side)), device_id_type=MESH)
-
-    @pl.when(gathering)
+        greet(gatherer(row))
+
+    @pl.when(active & gathers)
     def _():
-        for i in range(1, GROUPS):
-            there = served * TGC + (TGC - 1) * side
-            pl.semaphore_signal(barrier, inc=1, device_id=((k + i) % GROUPS, there), device_id_type=MESH)
+        for far in range(2):
+            greet(served * TGC + (TGC - 1) * far)
 
     def send(src, dst, ssem, rsem, dev):
         pltpu.make_async_remote_copy(
@@ -108,6 +116,9 @@
 
     def await_bytes(ref, sem):
         pltpu.make_async_copy(ref, ref, sem).wait()
+
+    def reorder(cells):
+        return jnp.dot(order[...], cells, preferred_element_type=F32)
 
     def mine(f):
         return jnp.minimum(2 * k + f, FACES - 1)
@@ -145,18 +156,16 @@
                 w = slots[n][1]
                 h = w % 2
                 at = 6 * e + 3 * o + i if e < 2 else 12 + 4 * (e - 2) + 2 * o + i // 2
-                for far in range(2):
-                    yield True, None, n, cr.at[x, at], crsem.at[x], 24 * far + w
-                for far in range(2):
-                    tile = gatherer(w // 2, far)
-                    if e >= 2:
-                        yield False, None, n, cc.at[x, h, 8 + 4 * (e - 2) + 2 * o + i // 2], ccsem.at[x], tile
-                    elif i == 0:
-                        yield False, h == 1, n, cc.at[x, 1, 4 * e + 2 * o], ccsem.at[x], tile
-                    elif i == 1:
-                        yield False, None, n, cc.at[x, h, 4 * e + 2 * o + h], ccsem.at[x], tile
-                    else:
-                        yield False, h == 0, n, cc.at[x, 0, 4 * e + 2 * o + 1], ccsem.at[x], tile
+                yield True, None, n, cr.at[x, at], crsem.at[x], aligner(w)
+                tile = gatherer(w // 2)
+                if e >= 2:
+                    yield False, None, n, cc.at[x, h, 8 + 4 * (e - 2) + 2 * o + i // 2], ccsem.at[x], tile
+                elif i == 0:
+                    yield False, h == 1, n, cc.at[x, 1, 4 * e + 2 * o], ccsem.at[x], tile
+                elif i == 1:
+                    yield False, None, n, cc.at[x, h, 4 * e + 2 * o + h], ccsem.at[x], tile
+                else:
+                    yield False, h == 0, n, cc.at[x, 0, 4 * e + 2 * o + 1], ccsem.at[x], tile
 
     def exchange_send(x, v):
         for f in range(2):
@@ -216,9 +225,6 @@
                         def _():
                             await_bytes(s1.at[x, n], s1sem.at[x, e])
 
-                if e < 2:
-                    await_bytes(s2r.at[x, 0:5], s2sem.at[x, 0])
-
             @pl.when(jnp.logical_not(edges[e]))
             def _():
                 await_bytes(s1.at[x, first : first + (3 if e < 2 else 2)], s1sem.at[x, e])
@@ -226,6 +232,11 @@
         @pl.when(gathers)
         def _():
             await_bytes(s2c.at[x], s2sem.at[x, 1])
+
+        @pl.when(lines_up)
+        def _():
+            await_bytes(s2r.at[x, 0], s2sem.at[x, 0])
+            await_bytes(s2r.at[x, 1, 0:5], s2sem.at[x, 0])
 
     def collect(x):
         def lines(buf, row_first, row_count, col_first):
@@ -244,34 +255,44 @@
             at = pick_at[face, e]
             return line[at // 2, at % 2]
 
-        for e in range(2):
-            @pl.when(edges[e])
-            def _():
-                await_bytes(cr.at[x], crsem.at[x])
-                lines(cr.at[x], lambda e, o: 6 * e + 3 * o, 3, lambda e, o: 12 + 4 * (e - 2) + 2 * o)
+        @pl.when(lines_up)
+        def _():
+            await_bytes(cr.at[x], crsem.at[x])
+            lines(cr.at[x], lambda e, o: 6 * e + 3 * o, 3, lambda e, o: 12 + 4 * (e - 2) + 2 * o)
+            for e in range(2):
+                tile = (TILES - TGC) * e + col
                 for g in range(GROUPS):
                     for f in range(2):
-                        s2r[x, g, f] = pick(2 * g + f, e)
-                d2r[x, k] = s2r[x, k]
+                        s2r[x, e, g, f] = pick(2 * g + f, e)
                 for i in range(1, GROUPS):
                     g = (k + i) % GROUPS
-                    send(s2r.at[x, g], d2r.at[x, k], s2sem.at[x, 0], d2sem.at[x, 0], (g, t))
+                    send(s2r.at[x, e, g], d2r.at[x, k], s2sem.at[x, 0], d2sem.at[x, 0], (g, tile))
+
+                @pl.when(tile != t)
+                def _():
+                    send(s2r.at[x, e, k], d2r.at[x, k], s2sem.at[x, 0], d2sem.at[x, 0], (k, tile))
+
+                @pl.when(tile == t)
+                def _():
+                    pltpu.make_async_copy(s2r.at[x, e, k], d2r.at[x, k], d2sem.at[x, 0]).start()
 
         @pl.when(gathers)
         def _():
             await_bytes(cc.at[x], ccsem.at[x])
             for h in range(2):
                 lines(cc.at[x, h], lambda e, o: 4 * e + 2 * o, 2, lambda e, o: 8 + 4 * (e - 2) + 2 * o)
-                for g in range(GROUPS):
-                    for f in range(2):
-                        s2c[x, g, h, f] = pick(2 * g + f, 2 + side)
+                for far in range(2):
+                    for g in range(GROUPS):
+                        for f in range(2):
+                            s2c[x, far, g, h, f] = pick(2 * g + f, 2 + far)
             for i in range(GROUPS):
                 g = (k + i) % GROUPS
-                there = served * TGC + (TGC - 1) * side
-                send(s2c.at[x, g], d2c.at[x, k], s2sem.at[x, 1], d2sem.at[x, 1], (g, there))
+                for far in range(2):
+                    there = served * TGC + (TGC - 1) * far
+                    send(s2c.at[x, far, g], d2c.at[x, k], s2sem.at[x, 1], d2sem.at[x, 1], (g, there))
 
     def arrived(x, e, f, h=0):
-        group = nbr[mine(f), e] // 2
+        group = nbr[e, mine(f)] // 2
         out = None
         for g in range(GROUPS):
             win = d2r[x, g, f] if e < 2 else d2c[x, g, h, f]
@@ -338,7 +359,7 @@
             @pl.when(edges[e])
             def _():
                 if e < 2:
-                    await_bytes(d2r.at[x, 0:5], d2sem.at[x, 0])
+                    await_bytes(d2r.at[x], d2sem.at[x, 0])
                 else:
                     await_bytes(d2c.at[x], d2sem.at[x, 1])
                 size = 16 if e < 2 else 32
@@ -365,7 +386,7 @@
 
     def backward_taps(l):
         def weights(f, e):
-            code = trn[mine(f), e]
+            code = trn[e, mine(f)]
             other, rev = code % 4, code // 4
             first = jnp.where(other == 1, 6, jnp.where(other == 3, 2, 0))
             step = jnp.where(other < 2, 1, 3)
@@ -444,8 +465,8 @@
     fetches = [
         pltpu.make_async_copy(src, dst, insem.at[n])
         for n, (src, dst) in enumerate((
-            (act_h.at[:, 0], act), (w1_h, wst.at[0]), (spread_h, spread), (nbr_h, nbr), (trn_h, trn),
-            (w2_h, wst.at[1]), (w3_h, wst.at[2]), (cot_h.at[:, 0], cot),
+            (act_h, act), (w1_h, wst.at[0]), (spread_h, spread), (nbr_h, nbr), (trn_h, trn),
+            (w2_h, wst.at[1]), (w3_h, wst.at[2]), (cot_h, cot),
         ))
     ]
 
@@ -453,20 +474,30 @@
     def _():
         for fetch in fetches:
             fetch.start()
+        place = lax.broadcasted_iota(jnp.int32, (CELLS, TW * TH), 0)
+        given = lax.broadcasted_iota(jnp.int32, (CELLS, TW * TH), 1)
+        order[...] = jnp.where((given % TH) * PITCH + given // TH == place, 1.0, 0.0).astype(BF)
         build_sel()
         z[...] = jnp.zeros_like(z)
         up[...] = jnp.zeros_like(up)
         sg[...] = jnp.zeros_like(sg)
         fetches[0].wait()
         for f in range(2):
-            for y in range(TH):
-                z[0, f, y * PITCH : y * PITCH + TW] = act[f, y]
-
-    @pl.when(glued | gathering)
+            z[0, f, :CELLS] = reorder(act[f]).astype(BF)
+
+    across, along = edges[0] | edges[1], edges[2] | edges[3]
+    most = active & ((across & along) | gathers)
+    some = active & (across ^ along)
+
+    @pl.when(most)
+    def _():
+        pl.semaphore_wait(barrier, 38 + 2 * (GROUPS - 1))
+
+    @pl.when(some)
     def _():
         pl.semaphore_wait(barrier, 38 + GROUPS - 1)
 
-    @pl.when(jnp.logical_not(glued | gathering))
+    @pl.when(jnp.logical_not(most | some))
     def _():
         pl.semaphore_wait(barrier, 38)
 
@@ -482,8 +513,8 @@
                     fetch.wait()
                 for face in range(FACES):
                     for e in range(4):
-                        code = trn[face, e]
-                        pick_at[face, e] = (code % 4) * 4 + (code // 4) * 2 + nbr[face, e] % 2
+                        code = trn[e, face]
+                        pick_at[face, e] = (code % 4) * 4 + (code // 4) * 2 + nbr[e, face] % 2
 
             @pl.when(l > 0)
             def _():
@@ -508,9 +539,7 @@
                 z[l + 1, f, :CELLS] = hidden.astype(BF)
 
         for f in range(2):
-            up[f] = jnp.zeros((CELLS, C), F32)
-            for y in range(TH):
-                up[f, y * PITCH : y * PITCH + TW] = cot[f, y].astype(F32)
+            up[f] = reorder(cot[f])
 
         @pl.loop(0, 3)
         def _(i):
@@ -577,7 +606,9 @@
             correct(x, backward_taps(l))
 
         for f in range(2):
-            gin[f] = up[f].astype(BF)
+            gin[f] = lax.dot_general(
+                order[...], up[f].astype(BF), (((0,), (0,)), ((), ())), preferred_element_type=F32
+            ).astype(BF)
         reduce_last(0)
 
         @pl.loop(0, 6)
@@ -597,24 +628,28 @@
 
 
 def shards(activation, cotangent, weight_one, weight_two, weight_three, neighbor, turn):
+    def flipped(field):
+        return field.transpose(0, 1, 3, 2, 4).reshape(2, TW * TH, C)
+
     vmem = pl.BlockSpec(memory_space=pltpu.VMEM)
     hbm = pl.BlockSpec(memory_space=pltpu.HBM)
     dma = pltpu.SemaphoreType.DMA
     gin, grads = pl.pallas_call(
         kernel,
         out_shape=(
-            jax.ShapeDtypeStruct((2, CELLS, C), BF),
+            jax.ShapeDtypeStruct((2, TW * TH, C), BF),
             jax.ShapeDtypeStruct((3, 9 * C, C), BF),
         ),
         in_specs=[hbm] * 8,
         out_specs=(vmem, vmem),
         scratch_shapes=[
+            pltpu.SMEM((4, FACES), jnp.int32),
+            pltpu.SMEM((4, FACES), jnp.int32),
             pltpu.SMEM((FACES, 4), jnp.int32),
-            pltpu.SMEM((FACES, 4), jnp.int32),
-            pltpu.SMEM((FACES, 4), jnp.int32),
-            pltpu.VMEM((2, TH, TW, C), BF),
-            pltpu.VMEM((2, TH, TW, C), BF),
+            pltpu.VMEM((2, TW * TH, C), BF),
+            pltpu.VMEM((2, TW * TH, C), BF),
             pltpu.VMEM((3 * ROWS, KZ), BF),
+            pltpu.VMEM((CELLS, TW * TH), BF),
             pltpu.VMEM((28 * 16, CELLS), BF),
             pltpu.VMEM((4, 2, KZ, C), BF),
             pltpu.VMEM((3, 2, ROWS, 3 * C), BF),
@@ -629,8 +664,8 @@
             pltpu.VMEM((6, 10, 2, 16, C), BF),
             pltpu.VMEM((6, 20, 2, 16, C), BF),
             pltpu.VMEM((6, 2, 16, 2, 16, C), BF),
-            pltpu.VMEM((6, GROUPS, 2, 16, C), BF),
-            pltpu.VMEM((6, GROUPS, 2, 2, 16, C), BF),
+            pltpu.VMEM((6, 2, GROUPS, 2, 16, C), BF),
+            pltpu.VMEM((6, 2, GROUPS, 2, 2, 16, C), BF),
             pltpu.VMEM((6, GROUPS, 2, 16, C), BF),
             pltpu.VMEM((6, GROUPS, 2, 2, 16, C), BF),
             pltpu.VMEM((3, 9 * C, C), BF),
@@ -649,14 +684,14 @@
             dma((3, 3)),
         ],
         compiler_params=pltpu.CompilerParams(
-            collective_id=0, has_side_effects=True, vmem_limit_bytes=48 * 1024 * 1024
+            collective_id=0, has_side_effects=True, vmem_limit_bytes=62 * 1024 * 1024
         ),
         name="glued_convolutions",
     )(
-        neighbor, turn, activation, cotangent, weight_one, weight_two, weight_three,
+        neighbor.T, turn.T, flipped(activation), flipped(cotangent), weight_one, weight_two, weight_three,
         jnp.asarray(spread_matrix(), BF),
     )
-    grad_input = gin.reshape(2, 1, TH, PITCH, C)[:, :, :, :TW]
+    grad_input = gin.reshape(2, 1, TW, TH, C).transpose(0, 1, 3, 2, 4)
     scaled = grads.reshape(3, 9, C, C).astype(F32) * (1.0 / math.sqrt(FACES * NS * NS))
     return grad_input, scaled[0], scaled[1], scaled[2]
 

time: 129 us -> 119 us (0.922)
  local copies, waits for them, and re-layouts: 9.56 us -> 1.91 us
  Pallas kernels: 119 us -> 115 us
    unnamed x13 -> x3, local copies, waits for them, and re-layouts: 8.31 us -> 0.67 us
    pallas_call x1, Pallas kernels: 119 us -> 115 us  [shards(): pl.pallas_call(kernel, out_shape=(jax.ShapeDtypeStruct((2, TW * TH, C), B...]
where the time goes in v4:
time: 119 us
  Pallas kernels  115 us (97%)
  local copies, waits for them, and re-layouts  1.91 us (2%)
  other arithmetic  1.3 us (1%)
    pallas_call x1, Pallas kernels, shards(): pl.pallas_call(kernel, out_shape=(jax.ShapeDtypeStruct((2, TW * TH, C), B...  115 us

profile of v4, /device:TPU:1, one launch (start us, length us, event | category | flops | bytes accessed | tf_op | source)
XLA Modules:
  0.0 119.3 jit_solution(9967169751960159849)
XLA Ops:
  0.6 115.4 %glued_convolutions.1 = (bf16[2,288,128]{2,1,0:T(8,128)(2,1)}, bf16[3,1152,128]{2,1,0:T(8,128)(2,1)}) custom-call(s32[4,12]{1,0:T(4,128)} %bitcast.22, s32[4,12]{1,0:T(4,128)} %bitcast.23, bf16[2,288,128]{2,1,0:T(8,128)(2,1)} %bitcast.19, bf16[2,288,128]{2,1,0:T(8,128)(2,1)} %bitcast.20, bf16[9,128,128]{2,1,0:T(8,128)(2,1)} %w1_h.1, ...), custom_call_target="tpu_custom_call" | custom-call | tf_op jit(solution)/shard_map/glued_convolutions/pallas_call | solution.py:637
  116.1 1.3 %convert_multiply_fusion = f32[3,1152,128]{2,1,0:T(8,128)S(1)} fusion(bf16[3,1152,128]{2,1,0:T(8,128)(2,1)} %get-tuple-element.7), kind=kLoop, calls=%fused_computation | loop fusion | flops 884736 | bytes 2654208 | tf_op jit(solution)/shard_map/mul | solution.py:695
  117.4 0.0 copy-start
  117.4 1.2 %fusion = (f32[1,1152,128]{2,1,0:T(8,128)}, f32[1,1152,128]{2,1,0:T(8,128)}, f32[1,1152,128]{2,1,0:T(8,128)}) fusion(f32[3,1152,128]{2,1,0:T(8,128)S(1)} %convert_multiply_fusion), kind=kLoop, calls=%fused_computation.1 | loop fusion | bytes 3538944 | tf_op jit(solution)/shard_map/slice | solution.py:696
  118.6 0.0 copy-done
  118.6 0.7 copy.14
Async XLA Ops:
  117.4 1.3 %copy-start = (bf16[2,288,128]{2,1,0:T(8,128)(2,1)S(1)}, bf16[2,288,128]{2,1,0:T(8,128)(2,1)}, u32[]{:S(2)}) copy-start(bf16[2,288,128]{2,1,0:T(8,128)(2,1)} %get-tuple-element.6) | copy-start | bytes 442372

commit v5 on v4

--- a/solution.py
+++ b/solution.py
@@ -73,8 +73,9 @@
     active = k < GROUPS
     owner = t < OWNERS
     edges = (row == 0, row == TGR - 1, col == 0, col == TGC - 1)
-    gathers = (row >= 1) & (row <= 2) & ((col == 1) | (col == 6))
-    served = 2 * (row - 1) + (col - 1) // 5
+    gathers = (row >= 1) & (row <= 2) & (((col >= 1) & (col <= 2)) | ((col >= 5) & (col <= 6)))
+    served = 2 * (row - 1) + col // 4
+    part = (col - 1 + (col // 4) * (7 - 2 * col)) % 2
     lines_up = (edges[0] & (col % 2 == 0)) | (edges[1] & (col % 2 == 1))
 
     barrier = pltpu.get_barrier_semaphore()
@@ -85,8 +86,8 @@
     def _(i):
         pl.semaphore_signal(barrier, inc=1, device_id=(k, (t + i) % 32), device_id_type=MESH)
 
-    def gatherer(r):
-        return (1 + r // 2) * TGC + 1 + 5 * (r % 2)
+    def gatherer(r, h):
+        return (1 + r // 2) * TGC + 1 + h + (r % 2) * (5 - 2 * h)
 
     def aligner(w):
         return (w % 2) * (TILES - TGC) + w
@@ -102,7 +103,8 @@
 
     @pl.when(active & (edges[2] | edges[3]))
     def _():
-        greet(gatherer(row))
+        greet(gatherer(row, 0))
+        greet(gatherer(row, 1))
 
     @pl.when(active & gathers)
     def _():
@@ -157,15 +159,15 @@
                 h = w % 2
                 at = 6 * e + 3 * o + i if e < 2 else 12 + 4 * (e - 2) + 2 * o + i // 2
                 yield True, None, n, cr.at[x, at], crsem.at[x], aligner(w)
-                tile = gatherer(w // 2)
+                tile = gatherer(w // 2, h)
                 if e >= 2:
-                    yield False, None, n, cc.at[x, h, 8 + 4 * (e - 2) + 2 * o + i // 2], ccsem.at[x], tile
+                    yield False, None, n, cc.at[x, 8 + 4 * (e - 2) + 2 * o + i // 2], ccsem.at[x], tile
                 elif i == 0:
-                    yield False, h == 1, n, cc.at[x, 1, 4 * e + 2 * o], ccsem.at[x], tile
+                    yield False, h == 1, n, cc.at[x, 4 * e + 2 * o], ccsem.at[x], tile
                 elif i == 1:
-                    yield False, None, n, cc.at[x, h, 4 * e + 2 * o + h], ccsem.at[x], tile
+                    yield False, None, n, cc.at[x, 4 * e + 2 * o + h], ccsem.at[x], tile
                 else:
-                    yield False, h == 0, n, cc.at[x, 0, 4 * e + 2 * o + 1], ccsem.at[x], tile
+                    yield False, h == 0, n, cc.at[x, 4 * e + 2 * o + 1], ccsem.at[x], tile
 
     def exchange_send(x, v):
         for f in range(2):
@@ -279,17 +281,15 @@
         @pl.when(gathers)
         def _():
             await_bytes(cc.at[x], ccsem.at[x])
-            for h in range(2):
-                lines(cc.at[x, h], lambda e, o: 4 * e + 2 * o, 2, lambda e, o: 8 + 4 * (e - 2) + 2 * o)
-                for far in range(2):
-                    for g in range(GROUPS):
-                        for f in range(2):
-                            s2c[x, far, g, h, f] = pick(2 * g + f, 2 + far)
-            for i in range(GROUPS):
-                g = (k + i) % GROUPS
-                for far in range(2):
-                    there = served * TGC + (TGC - 1) * far
-                    send(s2c.at[x, far, g], d2c.at[x, k], s2sem.at[x, 1], d2sem.at[x, 1], (g, there))
+            lines(cc.at[x], lambda e, o: 4 * e + 2 * o, 2, lambda e, o: 8 + 4 * (e - 2) + 2 * o)
+            for far in range(2):
+                there = served * TGC + (TGC - 1) * far
+                for g in range(GROUPS):
+                    for f in range(2):
+                        s2c[x, far, g, f] = pick(2 * g + f, 2 + far)
+                for i in range(GROUPS):
+                    g = (k + i) % GROUPS
+                    send(s2c.at[x, far, g], d2c.at[x, k, part], s2sem.at[x, 1], d2sem.at[x, 1], (g, there))
 
     def arrived(x, e, f, h=0):
         group = nbr[e, mine(f)] // 2
@@ -364,16 +364,19 @@
                     await_bytes(d2c.at[x], d2sem.at[x, 1])
                 size = 16 if e < 2 else 32
                 for f in range(2):
-                    sg[0, 0:16] = arrived(x, e, f, 0).astype(F32)
+                    win = sg.at[2 * e + f]
+                    win[0:16] = arrived(x, e, f, 0).astype(F32)
                     if e >= 2:
-                        sg[1, 0:16] = arrived(x, e, f, 1).astype(F32)
-                        sg[0, 13:26] = sg[1, 1:14]
-                    else:
-                        sg[0, 16:32] = jnp.zeros((16, C), F32)
+                        win[48:64] = arrived(x, e, f, 1).astype(F32)
+                        win[13:26] = win[49:62]
+                moved = []
+                for f in range(2):
                     more = None
                     for s, weight in enumerate(weights(f, e)):
-                        part = jnp.dot(sg[0, s : s + size].astype(BF), weight, preferred_element_type=F32)
+                        part = jnp.dot(sg[2 * e + f, s : s + size].astype(BF), weight, preferred_element_type=F32)
                         more = part if more is None else more + part
+                    moved.append(more)
+                for f, more in enumerate(moved):
                     if e < 2:
                         at = 0 if e == 0 else CELLS - PITCH
                         up[f, at : at + 16] = up[f, at : at + 16] + more
@@ -486,18 +489,16 @@
             z[0, f, :CELLS] = reorder(act[f]).astype(BF)
 
     across, along = edges[0] | edges[1], edges[2] | edges[3]
-    most = active & ((across & along) | gathers)
-    some = active & (across ^ along)
-
-    @pl.when(most)
-    def _():
-        pl.semaphore_wait(barrier, 38 + 2 * (GROUPS - 1))
-
-    @pl.when(some)
-    def _():
-        pl.semaphore_wait(barrier, 38 + GROUPS - 1)
-
-    @pl.when(jnp.logical_not(most | some))
+    counts = ((active & across & along, 3), (active & ((along & jnp.logical_not(across)) | gathers), 2), (active & across & jnp.logical_not(along), 1))
+    extra = jnp.bool_(False)
+    for cond, n in counts:
+        extra = extra | cond
+
+        @pl.when(cond)
+        def _():
+            pl.semaphore_wait(barrier, 38 + n * (GROUPS - 1))
+
+    @pl.when(jnp.logical_not(extra))
     def _():
         pl.semaphore_wait(barrier, 38)
 
@@ -571,19 +572,23 @@
             def _():
                 reduce_send(l)
 
+            @pl.when(i > 0)
+            def _():
+                reduce_mid(l + 1)
+
             collect(x)
 
             @pl.when(i < 2)
             def _():
                 reduce_send(l)
 
+            @pl.when(i == 2)
+            def _():
+                reduce_mid(l)
+
             @pl.when(i > 0)
             def _():
-                reduce_mid(l + 1)
-
-            @pl.when(i > 1)
-            def _():
-                reduce_last(l + 2)
+                reduce_last(l + 1)
 
             halo_local(x, d)
             for f in range(2):
@@ -600,8 +605,7 @@
 
             @pl.when(i == 2)
             def _():
-                reduce_mid(l)
-                reduce_last(l + 1)
+                reduce_last(l)
 
             correct(x, backward_taps(l))
 
@@ -609,7 +613,6 @@
             gin[f] = lax.dot_general(
                 order[...], up[f].astype(BF), (((0,), (0,)), ((), ())), preferred_element_type=F32
             ).astype(BF)
-        reduce_last(0)
 
         @pl.loop(0, 6)
         def _(x):
@@ -658,14 +661,14 @@
             pltpu.VMEM((2, CELLS, C), F32),
             pltpu.VMEM((3, 9, C, C), BF),
             pltpu.VMEM((3, 9, C, C), BF),
-            pltpu.VMEM((2, 40, C), F32),
+            pltpu.VMEM((8, 64, C), F32),
             pltpu.VMEM((8, 2, 16, C), BF),
             pltpu.VMEM((6, 28, 2, 16, C), BF),
             pltpu.VMEM((6, 10, 2, 16, C), BF),
             pltpu.VMEM((6, 20, 2, 16, C), BF),
-            pltpu.VMEM((6, 2, 16, 2, 16, C), BF),
+            pltpu.VMEM((6, 16, 2, 16, C), BF),
             pltpu.VMEM((6, 2, GROUPS, 2, 16, C), BF),
-            pltpu.VMEM((6, 2, GROUPS, 2, 2, 16, C), BF),
+            pltpu.VMEM((6, 2, GROUPS, 2, 16, C), BF),
             pltpu.VMEM((6, GROUPS, 2, 16, C), BF),
             pltpu.VMEM((6, GROUPS, 2, 2, 16, C), BF),
             pltpu.VMEM((3, 9 * C, C), BF),

time: 119 us -> 112 us (0.941)
  Pallas kernels: 115 us -> 108 us
    pallas_call x1, Pallas kernels: 115 us -> 108 us  [shards(): pl.pallas_call(kernel, out_shape=(jax.ShapeDtypeStruct((2, TW * TH, C), B...]
where the time goes in v5:
time: 112 us; the launch traced here: 111 us
  Pallas kernels  108 us (96%)
  local copies, waits for them, and re-layouts  1.91 us (2%)
  other arithmetic  1.3 us (1%)
    pallas_call x1, Pallas kernels, shards(): pl.pallas_call(kernel, out_shape=(jax.ShapeDtypeStruct((2, TW * TH, C), B...  108 us

profile of v5, /device:TPU:1, one launch (start us, length us, event | category | flops | bytes accessed | tf_op | source)
XLA Modules:
  0.0 111.5 jit_solution(75837782658274714)
XLA Ops:
  0.6 107.6 %glued_convolutions.1 = (bf16[2,288,128]{2,1,0:T(8,128)(2,1)}, bf16[3,1152,128]{2,1,0:T(8,128)(2,1)}) custom-call(s32[4,12]{1,0:T(4,128)} %bitcast.22, s32[4,12]{1,0:T(4,128)} %bitcast.23, bf16[2,288,128]{2,1,0:T(8,128)(2,1)} %bitcast.19, bf16[2,288,128]{2,1,0:T(8,128)(2,1)} %bitcast.20, bf16[9,128,128]{2,1,0:T(8,128)(2,1)} %w1_h.1, ...), custom_call_target="tpu_custom_call" | custom-call | tf_op jit(solution)/shard_map/glued_convolutions/pallas_call | solution.py:640
  108.2 1.3 %convert_multiply_fusion = f32[3,1152,128]{2,1,0:T(8,128)S(1)} fusion(bf16[3,1152,128]{2,1,0:T(8,128)(2,1)} %get-tuple-element.7), kind=kLoop, calls=%fused_computation | loop fusion | flops 884736 | bytes 2654208 | tf_op jit(solution)/shard_map/mul | solution.py:698
  109.5 0.0 copy-start
  109.5 1.2 %fusion = (f32[1,1152,128]{2,1,0:T(8,128)}, f32[1,1152,128]{2,1,0:T(8,128)}, f32[1,1152,128]{2,1,0:T(8,128)}) fusion(f32[3,1152,128]{2,1,0:T(8,128)S(1)} %convert_multiply_fusion), kind=kLoop, calls=%fused_computation.1 | loop fusion | bytes 3538944 | tf_op jit(solution)/shard_map/slice | solution.py:699
  110.8 0.0 copy-done
  110.8 0.7 copy.14
Async XLA Ops:
  109.5 1.3 %copy-start = (bf16[2,288,128]{2,1,0:T(8,128)(2,1)S(1)}, bf16[2,288,128]{2,1,0:T(8,128)(2,1)}, u32[]{:S(2)}) copy-start(bf16[2,288,128]{2,1,0:T(8,128)(2,1)} %get-tuple-element.6) | copy-start | bytes 442372

commit v6 on v5

--- a/solution.py
+++ b/solution.py
@@ -50,13 +50,16 @@
     return out.reshape(3 * ROWS, KZ)
 
 
-def gelu_parts(x):
+def gelu(x):
+    c = math.sqrt(2.0 / math.pi)
+    return x * (0.5 * (1.0 + jnp.tanh(c * x * (1.0 + 0.044715 * (x * x)))))
+
+
+def gelu_slope(x):
     c = math.sqrt(2.0 / math.pi)
     sq = x * x
     t = jnp.tanh(c * x * (1.0 + 0.044715 * sq))
-    half = 0.5 * (1.0 + t)
-    slope = half + 0.5 * x * (1.0 - t * t) * (c * (1.0 + 3.0 * 0.044715 * sq))
-    return x * half, slope
+    return 0.5 * (1.0 + t) + 0.5 * x * (1.0 - t * t) * (c * (1.0 + 3.0 * 0.044715 * sq))
 
 
 def kernel(
@@ -72,6 +75,8 @@
     col = t % TGC
     active = k < GROUPS
     owner = t < OWNERS
+    spreads = owner & (t // (OWNERS // 2) == k % 2)
+    mate = k + 1 - 2 * (k % 2)
     edges = (row == 0, row == TGR - 1, col == 0, col == TGC - 1)
     gathers = (row >= 1) & (row <= 2) & (((col >= 1) & (col <= 2)) | ((col >= 5) & (col <= 6)))
     served = 2 * (row - 1) + col // 4
@@ -248,10 +253,10 @@
                         first, count = row_first(e, o), row_count
                     else:
                         first, count = col_first(e, o), 2
-                    total = buf[first].astype(F32)
+                    total = buf[first]
                     for n in range(1, count):
-                        total = total + buf[first + n].astype(F32)
-                    line[2 * e + o] = total.astype(BF)
+                        total = total + buf[first + n]
+                    line[2 * e + o] = total
 
         def pick(face, e):
             at = pick_at[face, e]
@@ -307,8 +312,7 @@
             def _():
                 await_bytes(nb.at[x, 3 * side : 3 * side + 3], nsem.at[x, side])
                 for f in range(2):
-                    total = nb[x, 3 * side, f].astype(F32) + nb[x, 3 * side + 1, f].astype(F32)
-                    v[f, at : at + 16] = (total + nb[x, 3 * side + 2, f].astype(F32)).astype(BF)
+                    v[f, at : at + 16] = nb[x, 3 * side, f] + nb[x, 3 * side + 1, f] + nb[x, 3 * side + 2, f]
 
             @pl.when(edges[side])
             def _():
@@ -421,12 +425,20 @@
             for s in range(31):
                 total = total + a1[l, s].astype(F32)
             pb[l] = total.astype(BF)
-            a2[l, k] = pb[l]
-            for i in range(1, 8):
-                send(pb.at[l], a2.at[l, k], arsem_s.at[l, 1], arsem_r.at[l, 1], ((k + i) % 8, t))
+            for i in range(1, 4):
+                there = (2 * (k // 2) + 2 * i) % 8 + t // (OWNERS // 2)
+                send(pb.at[l], a2.at[l, k], arsem_s.at[l, 1], arsem_r.at[l, 1], (there, t))
+
+            @pl.when(spreads)
+            def _():
+                a2[l, k] = pb[l]
+
+            @pl.when(jnp.logical_not(spreads))
+            def _():
+                send(pb.at[l], a2.at[l, k], arsem_s.at[l, 1], arsem_r.at[l, 1], (mate, t))
 
     def reduce_last(l):
-        @pl.when(owner)
+        @pl.when(spreads)
         def _():
             @pl.when(active)
             def _():
@@ -446,24 +458,43 @@
             def _(i):
                 send(gf.at[l, here], gf.at[l, here], arsem_s.at[l, 2], arsem_r.at[l, 2], (k, (t + i) % 32))
 
+    def reduce_swap(l):
+        here = (k % 2) * (OWNERS // 2) * CHUNK
+        half = gf.at[l, pl.ds(here, OWNERS // 2 * CHUNK)]
+
+        @pl.when(spreads)
+        def _():
+            await_bytes(gf.at[l, 0 : (OWNERS // 2 - 1) * CHUNK], arsem_r.at[l, 2])
+
+        @pl.when(jnp.logical_not(spreads))
+        def _():
+            await_bytes(gf.at[l, 0 : OWNERS // 2 * CHUNK], arsem_r.at[l, 2])
+
+        send(half, half, arsem_s.at[l, 3], arsem_r.at[l, 3], (mate, t))
+
     def reduce_drain(l):
-        @pl.when(owner)
-        def _():
-            await_bytes(gf.at[l, 0 : (OWNERS - 1) * CHUNK], arsem_r.at[l, 2])
+        await_bytes(gf.at[l, 0 : OWNERS // 2 * CHUNK], arsem_r.at[l, 3])
+        await_bytes(gf.at[l, 0 : OWNERS // 2 * CHUNK], arsem_s.at[l, 3])
+
+        @pl.when(spreads)
+        def _():
             await_bytes(a1.at[l], arsem_s.at[l, 2])
 
-            @pl.when(active)
-            def _():
-                await_bytes(gb.at[l, 0 : (OWNERS - 1) * CHUNK], arsem_s.at[l, 0])
-                await_bytes(a1.at[l, 0:7], arsem_s.at[l, 1])
-
-        @pl.when(jnp.logical_not(owner))
-        def _():
-            await_bytes(gf.at[l], arsem_r.at[l, 2])
-
-            @pl.when(active)
-            def _():
-                await_bytes(gb.at[l], arsem_s.at[l, 0])
+        @pl.when(active & owner)
+        def _():
+            await_bytes(gb.at[l, 0 : (OWNERS - 1) * CHUNK], arsem_s.at[l, 0])
+
+        @pl.when(active & jnp.logical_not(owner))
+        def _():
+            await_bytes(gb.at[l], arsem_s.at[l, 0])
+
+        @pl.when(active & spreads)
+        def _():
+            await_bytes(a1.at[l, 0:3], arsem_s.at[l, 1])
+
+        @pl.when(active & owner & jnp.logical_not(spreads))
+        def _():
+            await_bytes(a1.at[l, 0:4], arsem_s.at[l, 1])
 
     fetches = [
         pltpu.make_async_copy(src, dst, insem.at[n])
@@ -519,6 +550,8 @@
 
             @pl.when(l > 0)
             def _():
+                for f in range(2):
+                    slope[l - 1, f] = gelu_slope(up[f])
                 finish(l - 1)
 
             collect(l)
@@ -534,12 +567,14 @@
                     total = part if total is None else total + part
                 up[f] = total
             correct(l, forward_taps(l))
-            for f in range(2):
-                hidden, tilt = gelu_parts(up[f])
-                slope[l, f] = tilt
-                z[l + 1, f, :CELLS] = hidden.astype(BF)
+
+            @pl.when(l < 2)
+            def _():
+                for f in range(2):
+                    z[l + 1, f, :CELLS] = gelu(up[f]).astype(BF)
 
         for f in range(2):
+            slope[2, f] = gelu_slope(up[f])
             up[f] = reorder(cot[f])
 
         @pl.loop(0, 3)
@@ -625,7 +660,9 @@
         reduce_last(1)
         reduce_last(0)
 
-    for l in range(3):
+    for l in (2, 1, 0):
+        reduce_swap(l)
+    for l in (2, 1, 0):
         reduce_drain(l)
         grads[l] = gf[l]
 
@@ -683,8 +720,8 @@
             dma((6,)),
             dma((6, 2)),
             dma((6, 2)),
-            dma((3, 3)),
-            dma((3, 3)),
+            dma((3, 4)),
+            dma((3, 4)),
         ],
         compiler_params=pltpu.CompilerParams(
             collective_id=0, has_side_effects=True, vmem_limit_bytes=62 * 1024 * 1024

time: 112 us -> 109 us (0.973)
  Pallas kernels: 108 us -> 105 us
    pallas_call x1, Pallas kernels: 108 us -> 105 us  [shards(): pl.pallas_call(kernel, out_shape=(jax.ShapeDtypeStruct((2, TW * TH, C), B...]
where the time goes in v6:
time: 109 us; the launch traced here: 108 us
  Pallas kernels  105 us (96%)
  local copies, waits for them, and re-layouts  1.91 us (2%)
  other arithmetic  1.3 us (1%)
    pallas_call x1, Pallas kernels, shards(): pl.pallas_call(kernel, out_shape=(jax.ShapeDtypeStruct((2, TW * TH, C), B...  105 us

profile of v6, /device:TPU:1, one launch (start us, length us, event | category | flops | bytes accessed | tf_op | source)
XLA Modules:
  0.0 108.5 jit_solution(8677184315914934429)
XLA Ops:
  0.6 104.6 %glued_convolutions.1 = (bf16[2,288,128]{2,1,0:T(8,128)(2,1)}, bf16[3,1152,128]{2,1,0:T(8,128)(2,1)}) custom-call(s32[4,12]{1,0:T(4,128)} %bitcast.22, s32[4,12]{1,0:T(4,128)} %bitcast.23, bf16[2,288,128]{2,1,0:T(8,128)(2,1)} %bitcast.19, bf16[2,288,128]{2,1,0:T(8,128)(2,1)} %bitcast.20, bf16[9,128,128]{2,1,0:T(8,128)(2,1)} %w1_h.1, ...), custom_call_target="tpu_custom_call" | custom-call | tf_op jit(solution)/shard_map/glued_convolutions/pallas_call | solution.py:677
  105.3 1.3 %convert_multiply_fusion = f32[3,1152,128]{2,1,0:T(8,128)S(1)} fusion(bf16[3,1152,128]{2,1,0:T(8,128)(2,1)} %get-tuple-element.7), kind=kLoop, calls=%fused_computation | loop fusion | flops 884736 | bytes 2654208 | tf_op jit(solution)/shard_map/mul | solution.py:735
  106.6 0.0 copy-start
  106.6 1.2 %fusion = (f32[1,1152,128]{2,1,0:T(8,128)}, f32[1,1152,128]{2,1,0:T(8,128)}, f32[1,1152,128]{2,1,0:T(8,128)}) fusion(f32[3,1152,128]{2,1,0:T(8,128)S(1)} %convert_multiply_fusion), kind=kLoop, calls=%fused_computation.1 | loop fusion | bytes 3538944 | tf_op jit(solution)/shard_map/slice | solution.py:736
  107.8 0.0 copy-done
  107.8 0.7 copy.14
Async XLA Ops:
  106.6 1.3 %copy-start = (bf16[2,288,128]{2,1,0:T(8,128)(2,1)S(1)}, bf16[2,288,128]{2,1,0:T(8,128)(2,1)}, u32[]{:S(2)}) copy-start(bf16[2,288,128]{2,1,0:T(8,128)(2,1)} %get-tuple-element.6) | copy-start | bytes 442372

commit v7 on v6

--- a/solution.py
+++ b/solution.py
@@ -174,11 +174,12 @@
                 else:
                     yield False, h == 0, n, cc.at[x, 4 * e + 2 * o + 1], ccsem.at[x], tile
 
-    def exchange_send(x, v):
+    def cut_windows(x, v):
         for f in range(2):
             cut = jnp.dot(sel[...], v[f, :CELLS], preferred_element_type=F32)
             s1[x, :, f] = cut.astype(BF).reshape(28, 16, C)
 
+    def exchange_send(x):
         for e in range(4):
             @pl.when(edges[e])
             def _():
@@ -518,6 +519,7 @@
         fetches[0].wait()
         for f in range(2):
             z[0, f, :CELLS] = reorder(act[f]).astype(BF)
+        cut_windows(0, z.at[0])
 
     across, along = edges[0] | edges[1], edges[2] | edges[3]
     counts = ((active & across & along, 3), (active & ((along & jnp.logical_not(across)) | gathers), 2), (active & across & jnp.logical_not(along), 1))
@@ -537,7 +539,7 @@
     def _():
         @pl.loop(0, 3)
         def _(l):
-            exchange_send(l, z.at[l])
+            exchange_send(l)
 
             @pl.when(l == 0)
             def _():
@@ -572,6 +574,7 @@
             def _():
                 for f in range(2):
                     z[l + 1, f, :CELLS] = gelu(up[f]).astype(BF)
+                cut_windows(l + 1, z.at[l + 1])
 
         for f in range(2):
             slope[2, f] = gelu_slope(up[f])
@@ -584,7 +587,8 @@
             d = z.at[3]
             for f in range(2):
                 d[f, :CELLS] = (up[f] * slope[l, f]).astype(BF)
-            exchange_send(x, d)
+            cut_windows(x, d)
+            exchange_send(x)
 
             @pl.when(i == 0)
             def _():
@@ -649,10 +653,6 @@
                 order[...], up[f].astype(BF), (((0,), (0,)), ((), ())), preferred_element_type=F32
             ).astype(BF)
 
-        @pl.loop(0, 6)
-        def _(x):
-            sent(x)
-
     @pl.when(jnp.logical_not(active))
     def _():
         gin[...] = jnp.zeros_like(gin)
@@ -660,11 +660,21 @@
         reduce_last(1)
         reduce_last(0)
 
-    for l in (2, 1, 0):
-        reduce_swap(l)
-    for l in (2, 1, 0):
+    reduce_swap(2)
+    reduce_swap(1)
+
+    @pl.when(active)
+    def _():
+        @pl.loop(0, 6)
+        def _(x):
+            sent(x)
+
+    for l in (2, 1):
         reduce_drain(l)
         grads[l] = gf[l]
+    reduce_swap(0)
+    reduce_drain(0)
+    grads[0] = gf[0]
 
 
 def shards(activation, cotangent, weight_one, weight_two, weight_three, neighbor, turn):

time: 109 us -> 108 us (level)
  no operation moved by 1% of the time
where the time goes in v7:
time: 108 us
  Pallas kernels  104 us (96%)
  local copies, waits for them, and re-layouts  1.91 us (2%)
  other arithmetic  1.3 us (1%)
    pallas_call x1, Pallas kernels, shards(): pl.pallas_call(kernel, out_shape=(jax.ShapeDtypeStruct((2, TW * TH, C), B...  104 us

profile of v7, /device:TPU:1, one launch (start us, length us, event | category | flops | bytes accessed | tf_op | source)
XLA Modules:
  0.0 107.8 jit_solution(8630172895224881472)
XLA Ops:
  0.6 103.9 %glued_convolutions.1 = (bf16[2,288,128]{2,1,0:T(8,128)(2,1)}, bf16[3,1152,128]{2,1,0:T(8,128)(2,1)}) custom-call(s32[4,12]{1,0:T(4,128)} %bitcast.22, s32[4,12]{1,0:T(4,128)} %bitcast.23, bf16[2,288,128]{2,1,0:T(8,128)(2,1)} %bitcast.19, bf16[2,288,128]{2,1,0:T(8,128)(2,1)} %bitcast.20, bf16[9,128,128]{2,1,0:T(8,128)(2,1)} %w1_h.1, ...), custom_call_target="tpu_custom_call" | custom-call | tf_op jit(solution)/shard_map/glued_convolutions/pallas_call | solution.py:687
  104.6 1.3 %convert_multiply_fusion = f32[3,1152,128]{2,1,0:T(8,128)S(1)} fusion(bf16[3,1152,128]{2,1,0:T(8,128)(2,1)} %get-tuple-element.7), kind=kLoop, calls=%fused_computation | loop fusion | flops 884736 | bytes 2654208 | tf_op jit(solution)/shard_map/mul | solution.py:745
  105.9 0.0 copy-start
  105.9 1.2 %fusion = (f32[1,1152,128]{2,1,0:T(8,128)}, f32[1,1152,128]{2,1,0:T(8,128)}, f32[1,1152,128]{2,1,0:T(8,128)}) fusion(f32[3,1152,128]{2,1,0:T(8,128)S(1)} %convert_multiply_fusion), kind=kLoop, calls=%fused_computation.1 | loop fusion | bytes 3538944 | tf_op jit(solution)/shard_map/slice | solution.py:746
  107.1 0.0 copy-done
  107.1 0.7 copy.14
Async XLA Ops:
  105.9 1.3 %copy-start = (bf16[2,288,128]{2,1,0:T(8,128)(2,1)S(1)}, bf16[2,288,128]{2,1,0:T(8,128)(2,1)}, u32[]{:S(2)}) copy-start(bf16[2,288,128]{2,1,0:T(8,128)(2,1)} %get-tuple-element.6) | copy-start | bytes 442372

commit v8 on v7

--- a/solution.py
+++ b/solution.py
@@ -549,6 +549,9 @@
                     for e in range(4):
                         code = trn[e, face]
                         pick_at[face, e] = (code % 4) * 4 + (code // 4) * 2 + nbr[e, face] % 2
+                for n in range(3):
+                    for tap in range(9):
+                        wbk[n, tap] = wst[n, tap].astype(F32).T.astype(BF)
 
             @pl.when(l > 0)
             def _():
@@ -593,9 +596,6 @@
             @pl.when(i == 0)
             def _():
                 finish(2)
-                for n in range(3):
-                    for tap in range(9):
-                        wbk[n, tap] = wst[n, tap].astype(F32).T.astype(BF)
 
             for dy in range(3):
                 total = None

time: 108 us -> 108 us (level)
  no operation moved by 1% of the time
where the time goes in v8:
time: 108 us
  Pallas kernels  104 us (96%)
  local copies, waits for them, and re-layouts  1.91 us (2%)
  other arithmetic  1.3 us (1%)
    pallas_call x1, Pallas kernels, shards(): pl.pallas_call(kernel, out_shape=(jax.ShapeDtypeStruct((2, TW * TH, C), B...  104 us

profile of v8, /device:TPU:1, one launch (start us, length us, event | category | flops | bytes accessed | tf_op | source)
XLA Modules:
  0.0 108.2 jit_solution(4031249455681689331)
XLA Ops:
  0.6 104.3 %glued_convolutions.1 = (bf16[2,288,128]{2,1,0:T(8,128)(2,1)}, bf16[3,1152,128]{2,1,0:T(8,128)(2,1)}) custom-call(s32[4,12]{1,0:T(4,128)} %bitcast.22, s32[4,12]{1,0:T(4,128)} %bitcast.23, bf16[2,288,128]{2,1,0:T(8,128)(2,1)} %bitcast.19, bf16[2,288,128]{2,1,0:T(8,128)(2,1)} %bitcast.20, bf16[9,128,128]{2,1,0:T(8,128)(2,1)} %w1_h.1, ...), custom_call_target="tpu_custom_call" | custom-call | tf_op jit(solution)/shard_map/glued_convolutions/pallas_call | solution.py:687
  105.0 1.3 %convert_multiply_fusion = f32[3,1152,128]{2,1,0:T(8,128)S(1)} fusion(bf16[3,1152,128]{2,1,0:T(8,128)(2,1)} %get-tuple-element.7), kind=kLoop, calls=%fused_computation | loop fusion | flops 884736 | bytes 2654208 | tf_op jit(solution)/shard_map/mul | solution.py:745
  106.3 0.0 copy-start
  106.3 1.2 %fusion = (f32[1,1152,128]{2,1,0:T(8,128)}, f32[1,1152,128]{2,1,0:T(8,128)}, f32[1,1152,128]{2,1,0:T(8,128)}) fusion(f32[3,1152,128]{2,1,0:T(8,128)S(1)} %convert_multiply_fusion), kind=kLoop, calls=%fused_computation.1 | loop fusion | bytes 3538944 | tf_op jit(solution)/shard_map/slice | solution.py:746
  107.5 0.0 copy-done
  107.5 0.7 copy.14
Async XLA Ops:
  106.3 1.3 %copy-start = (bf16[2,288,128]{2,1,0:T(8,128)(2,1)S(1)}, bf16[2,288,128]{2,1,0:T(8,128)(2,1)}, u32[]{:S(2)}) copy-start(bf16[2,288,128]{2,1,0:T(8,128)(2,1)} %get-tuple-element.6) | copy-start | bytes 442372
